TPU v7x, 512 devices: a whole 4x8x8 slice. The times are simulated.
512 devices in a mesh: dp: 32 (over y, x), expert: 16 (over z, core).
Axes of the slice: x: 4, y: 8, z: 8, core: 2. Of those that a mesh axis runs over, the one named last changes fastest.
Arguments:
- tokens: bfloat16 [1024, 7168], P(('dp', 'expert')), may hold values from -6 to 6
- w_gate: bfloat16 [16, 7168, 1024], P('expert', 'dp'), may hold values from -0.0625 to 0.0625
- w_up: bfloat16 [16, 7168, 1024], P('expert', 'dp'), may hold values from -0.0625 to 0.0625
- w_down: bfloat16 [16, 1024, 7168], P('expert', None, 'dp'), may hold values from -0.1875 to 0.1875
- routes: int32 [1024, 8], P(('dp', 'expert')), may hold values from 0 to 15, all different within a row; in each aligned block of 2 rows (0 to 1, 2 to 3, ...) at most 2 rows name the same one
- scores: float32 [1024, 8], P(('dp', 'expert')), may hold values from 0.1 to 1
Outputs:
- mixed: bfloat16 [1024, 7168], P(('dp', 'expert'))
Inputs may be any that keep to these rules, and one draw needn't show every extreme that they name: `routes`: in the rows of one device no expert is named more than 2 times, a bound that some block reaches there; a request names 8 different experts.
All inputs are finite; a program needn't handle non-finite values.
Results may differ from a plain program's by a relative error of at most 0.034.
Values may be sent and summed in bfloat16 or wider, within the bound.
A program may use at most 64 MiB of HBM per device.

v0:
```python
import jax
import jax.numpy as jnp
from jax import lax
from jax.sharding import PartitionSpec as P

route_scale = 2.5


def slot_targets(routes, experts, capacity):
    flat_routes = routes.reshape(-1)
    hits = (flat_routes[:, None] == jnp.arange(experts, dtype=jnp.int32)[None, :]).astype(jnp.int32)
    before = jnp.cumsum(hits, axis=0) - hits
    position = jnp.sum(before * hits, axis=1)
    return flat_routes * capacity + position


def shards(tokens, w_gate, w_up, w_down, routes, scores):
    dp_count = lax.axis_size("dp")
    experts = lax.axis_size("expert")
    requests, width = tokens.shape
    topk = routes.shape[1]
    capacity = min(requests, max(2, 2 * requests * topk // experts))
    slice_width = width // dp_count
    targets = slot_targets(routes, experts, capacity)
    placing = (targets[None, :] == jnp.arange(experts * capacity, dtype=jnp.int32)[:, None]).astype(
        jnp.bfloat16
    )
    repeated = jnp.repeat(tokens, topk, axis=0)
    outgoing = jnp.dot(placing, repeated, preferred_element_type=jnp.float32).astype(jnp.bfloat16)
    outgoing = outgoing.reshape(experts, capacity, dp_count, slice_width)
    arrived = lax.all_to_all(
        lax.all_to_all(outgoing, "dp", split_axis=2, concat_axis=2, tiled=True),
        "expert",
        split_axis=0,
        concat_axis=0,
        tiled=True,
    )
    slot_rows = arrived.reshape(-1, slice_width)
    gate_local = w_gate[0]
    up_local = w_up[0]
    down_local = w_down[0]
    gate_part = jnp.dot(slot_rows, gate_local, preferred_element_type=jnp.float32)
    up_part = jnp.dot(slot_rows, up_local, preferred_element_type=jnp.float32)
    gate_sum, up_sum = (
        lax.psum(gate_part.astype(jnp.bfloat16), "dp").astype(jnp.float32),
        lax.psum(up_part.astype(jnp.bfloat16), "dp").astype(jnp.float32),
    )
    hidden = (jax.nn.silu(gate_sum) * up_sum).astype(jnp.bfloat16)
    expert_out = jnp.dot(hidden, down_local, preferred_element_type=jnp.float32).astype(
        jnp.bfloat16
    )
    returning = expert_out.reshape(experts, capacity, dp_count, slice_width)
    replies = lax.all_to_all(
        lax.all_to_all(returning, "dp", split_axis=2, concat_axis=2, tiled=True),
        "expert",
        split_axis=0,
        concat_axis=0,
        tiled=True,
    )
    replies = replies.reshape(experts * capacity, width)
    picked = jnp.take(replies, targets, axis=0).reshape(requests, topk, width)
    weights = route_scale * scores / jnp.sum(scores, axis=1, keepdims=True)
    combined = jnp.einsum("rk,rkd->rd", weights, picked.astype(jnp.float32))
    return combined.astype(jnp.bfloat16)


def solution(mesh):
    placed = (
        P(("dp", "expert"), None),
        P("expert", "dp", None),
        P("expert", "dp", None),
        P("expert", None, "dp"),
        P(("dp", "expert"), None),
        P(("dp", "expert"), None),
    )
    return jax.shard_map(
        shards, mesh=mesh, in_specs=placed, out_specs=P(("dp", "expert"), None), check_vma=False
    )
```

profile of v0, /device:TPU:1, one launch (start us, length us, event | category | flops | bytes accessed | tf_op | source)
XLA Modules:
  0.0 299.8 jit_solution(15548182319487154487)
XLA Ops:
  6.5 0.8 reshape.70
  7.5 0.2 select_reduce_fusion
  7.7 1.0 convolution_convert_fusion
  8.7 0.7 reshape.72
  9.4 0.5 copy.18
  10.0 26.6 %all_to_all.20 = bf16[16,2,32,224]{3,1,0,2:T(2,128)(2,1)S(1)} all-to-all(bf16[16,2,32,224]{3,1,0,2:T(2,128)(2,1)S(1)} %copy.18), channel_id=1, replica_groups=mesh['dp'=32,'expert'=16] {'dp'}, dimensions={2} | all-to-all | bytes 917504 | tf_op jit(solution)/shard_map/all_to_all | solution.py:32
  36.6 0.5 copy.19
  37.1 29.8 %all_to_all.21 = bf16[16,2,32,224]{3,1,2,0:T(2,128)(2,1)S(1)} all-to-all(bf16[16,2,32,224]{3,1,2,0:T(2,128)(2,1)S(1)} %copy.19), channel_id=1, replica_groups=mesh['dp'=32,'expert'=16] {'expert'}, dimensions={0} | all-to-all | bytes 917504 | tf_op jit(solution)/shard_map/all_to_all | solution.py:31
  66.9 0.1 copy.20
  67.0 2.0 convolution_convert_fusion.1
  69.0 2.0 convolution_convert_fusion.2
  71.1 164.2 %all-reduce.3.cloned.1.call-done = (bf16[1024,1024]{1,0:T(8,128)(2,1)}, bf16[1024,1024]{1,0:T(8,128)(2,1)}) async-done(((bf16[1024,1024]{1,0:T(8,128)(2,1)}, bf16[1024,1024]{1,0:T(8,128)(2,1)}), (bf16[1024,1024]{1,0:T(8,128)(2,1)}, bf16[1024,1024]{1,0:T(8,128)(2,1)})) %all-reduce.3.cloned.1.call-update) | async-done | bytes 4194320 | tf_op jit(solution)/shard_map/psum | solution.py:46
  235.3 3.8 %fusion.7 = bf16[1024,224]{0,1:T(8,128)(2,1)S(1)} fusion(bf16[1024,1024]{1,0:T(8,128)(2,1)} %get-tuple-element.5, bf16[1024,1024]{1,0:T(8,128)(2,1)} %get-tuple-element.6, bf16[1,1024,224]{1,2,0:T(8,128)(2,1)S(1)} %copy-done.4), kind=kOutput, calls=%fused_computation.12 | convolution fusion | flops 478380032 | bytes 5111808 | tf_op jit(solution)/shard_map/dot_general | solution.py:49
  239.1 0.2 copy.21
  239.3 0.5 copy.22
  239.8 19.0 %all_to_all.22 = bf16[16,2,32,224]{3,1,0,2:T(2,128)(2,1)S(1)} all-to-all(bf16[16,2,32,224]{3,1,0,2:T(2,128)(2,1)S(1)} %copy.22), channel_id=1, replica_groups=mesh['dp'=32,'expert'=16] {'dp'}, dimensions={2} | all-to-all | bytes 917504 | tf_op jit(solution)/shard_map/all_to_all | solution.py:54
  258.9 1.3 copy.23
  260.2 12.9 %all-to-all-start.3 = ((bf16[16,2,32,224]{3,1,2,0:T(2,128)(2,1)}), bf16[16,2,32,224]{3,1,2,0:T(2,128)(2,1)S(1)}, u32[]{:S(2)}, u32[]{:S(2)}) async-start(bf16[16,2,32,224]{3,1,2,0:T(2,128)(2,1)} %copy.23), calls=%async_computation.3 | async-start | bytes 1048576 | tf_op jit(solution)/shard_map/all_to_all | solution.py:53
  273.3 0.1 reduce_sum.22
  273.5 16.9 %all-to-all-done.3 = bf16[16,2,32,224]{3,1,2,0:T(2,128)(2,1)S(1)} async-done(((bf16[16,2,32,224]{3,1,2,0:T(2,128)(2,1)}), bf16[16,2,32,224]{3,1,2,0:T(2,128)(2,1)S(1)}, u32[]{:S(2)}, u32[]{:S(2)}) %all-to-all-start.3) | async-done | bytes 458784 | tf_op jit(solution)/shard_map/all_to_all | solution.py:53
  290.5 0.9 reshape.75
  291.3 0.7 gather_fusion
  292.0 0.3 fusion.13
  292.3 0.6 copy.28
  (23 shorter events, 0.5 us)
Async XLA Ops:
  6.5 60.4 %copy-start = (bf16[1,224,1024]{2,1,0:T(8,128)(2,1)S(1)}, bf16[1,224,1024]{2,1,0:T(8,128)(2,1)}, u32[]{:S(2)}) copy-start(bf16[1,224,1024]{2,1,0:T(8,128)(2,1)} %param.8) | copy-start | bytes 1376260
  6.5 228.7 %all-reduce.3.cloned.1.call-start = ((), (), s32[]{:S(2)}) async-start(), calls=%async_computation.4 | async-start | bytes 8388608 | tf_op jit(solution)/shard_map/psum | solution.py:46
  66.9 2.1 copy-start.1
  71.1 164.2 %copy-start.4 = (bf16[1,1024,224]{1,2,0:T(8,128)(2,1)S(1)}, bf16[1,1024,224]{1,2,0:T(8,128)(2,1)}, u32[]{:S(2)}) copy-start(bf16[1,1024,224]{1,2,0:T(8,128)(2,1)} %param.9) | copy-start | bytes 1376260
  239.3 33.8 %copy-start.2 = (s32[2,8]{1,0:T(2,128)S(1)}, s32[2,8]{1,0:T(2,128)}, u32[]{:S(2)}) copy-start(s32[2,8]{1,0:T(2,128)} %param.10) | copy-start | bytes 196
  239.3 34.0 %copy-start.3 = (f32[2,8]{1,0:T(2,128)S(1)}, f32[2,8]{1,0:T(2,128)}, u32[]{:S(2)}) copy-start(f32[2,8]{1,0:T(2,128)} %param.11) | copy-start | bytes 196
  260.2 30.2 %all-to-all-start.3 = ((bf16[16,2,32,224]{3,1,2,0:T(2,128)(2,1)}), bf16[16,2,32,224]{3,1,2,0:T(2,128)(2,1)S(1)}, u32[]{:S(2)}, u32[]{:S(2)}) async-start(bf16[16,2,32,224]{3,1,2,0:T(2,128)(2,1)} %copy.23), calls=%async_computation.3 | async-start | bytes 1048576 | tf_op jit(solution)/shard_map/all_to_all | solution.py:53
Sparse Core Ops, SparseCore 0:
  71.2 163.9 all-reduce.2
where the time goes:
time: 300 us
  waiting for transfers between devices  181 us (60%)
  blocking collectives  75.4 us (25%)
  between operations  13.5 us (4%)
  starting transfers between devices  12.9 us (4%)
  matrix products  9.15 us (3%)
  local copies, waits for them, and re-layouts  7.16 us (2%)
    psum x1, waiting for transfers between devices, shards(): lax.psum(up_part.astype(jnp.bfloat16), 'dp').astype(jnp.float32)  164 us
    all_to_all x1, blocking collectives, shards(): lax.all_to_all(lax.all_to_all(outgoing, 'dp', split_axis=2, concat_axis=2...  29.8 us
    all_to_all x1, blocking collectives, shards(): lax.all_to_all(outgoing, 'dp', split_axis=2, concat_axis=2, tiled=True)  26.6 us
    all_to_all x1, blocking collectives, shards(): lax.all_to_all(returning, 'dp', split_axis=2, concat_axis=2, tiled=True)  19 us
    all_to_all x1, waiting for transfers between devices, shards(): lax.all_to_all(lax.all_to_all(returning, 'dp', split_axis=2, concat_axis=...  16.9 us
    all_to_all x1, starting transfers between devices, shards(): lax.all_to_all(lax.all_to_all(returning, 'dp', split_axis=2, concat_axis=...  12.9 us
  transfers between devices with their start and end apart: 2, of which 2 were waited for; matrix products, arithmetic and copies ran while one was open for 0% of the time, Pallas kernels for 0%

commit v1 on v0

v1 whole, which is shorter than its diff:
```python
import functools

import jax
import jax.numpy as jnp
from jax import lax
from jax.experimental import pallas as pl
from jax.experimental.pallas import tpu as pltpu
from jax.sharding import PartitionSpec as P

MESH = pl.DeviceIdType.MESH
F32 = jnp.float32
BF16 = jnp.bfloat16

ROUTE_SCALE = 2.5
NX, NY, NZ = 4, 8, 8
N_DP = NX * NY
N_EXPERT = 2 * NZ
D = 7168
WIDTH = D // N_DP
FFW = 1024
PAD = 256
ROWS = 64
CHUNK = 2 * ROWS
QUARTER = FFW // NX
STRIP = CHUNK // NY
OFFSETS = (0, 1, 7, 2, 6, 3, 5, 4)
BACK = tuple(OFFSETS.index((NZ - o) % NZ) for o in OFFSETS)
STAGGER = 1


def kernel(
    tok_ref, wg_hbm, wu_hbm, wd_hbm, out_ref,
    wg, wu, wd, mail, xall, part, xa, xy, xs, ya, yt, yx, hid, outs, got, back_src, back,
    load_sem, mail_sem, x_send, x_recv, rs_send, rs_recv, ag_send, ag_recv, o_send, o_recv, b_sem,
):
    dp = lax.axis_index("dp")
    e = lax.axis_index("expert")
    X, Y = dp % NX, dp // NX
    Z, C = e // 2, e % 2

    def at(x, y):
        return (lax.rem(y, NY) * NX + lax.rem(x, NX), e)

    loads = [
        pltpu.make_async_copy(wg_hbm.at[0], wg.at[pl.ds(0, WIDTH)], load_sem.at[0]),
        pltpu.make_async_copy(wu_hbm.at[0], wu.at[pl.ds(0, WIDTH)], load_sem.at[1]),
        pltpu.make_async_copy(wd_hbm.at[0], wd, load_sem.at[2]),
    ]
    for load in loads:
        load.start()

    barrier = pltpu.get_barrier_semaphore()

    def greet_dp(j, carry):
        pl.semaphore_signal(barrier, inc=1, device_id=((dp + j) % N_DP, e), device_id_type=MESH)
        return carry

    def greet_expert(j, carry):
        pl.semaphore_signal(barrier, inc=1, device_id=(dp, (e + j) % N_EXPERT), device_id_type=MESH)
        return carry

    lax.fori_loop(1, N_DP, greet_dp, 0)
    lax.fori_loop(1, N_EXPERT, greet_expert, 0)

    wg[pl.ds(WIDTH, PAD - WIDTH), :] = jnp.zeros((PAD - WIDTH, FFW), BF16)
    wu[pl.ds(WIDTH, PAD - WIDTH), :] = jnp.zeros((PAD - WIDTH, FFW), BF16)
    outs[...] = jnp.zeros_like(outs)

    pl.semaphore_wait(barrier, N_DP - 1 + N_EXPERT - 1)

    sends = []

    def send(src, dst, send_sem, recv_sem, device):
        copy = pltpu.make_async_remote_copy(src, dst, send_sem, recv_sem, device_id=device, device_id_type=MESH)
        copy.start()
        sends.append(copy)
        return copy

    def spread(src, dst, sems):
        own = pltpu.make_async_copy(src.at[dp], dst.at[dp], sems.at[1])
        own.start()

        def body(j, carry):
            d = (dp + j) % N_DP
            pltpu.make_async_remote_copy(
                src.at[d], dst.at[dp], sems.at[0], sems.at[1], device_id=(d, e), device_id_type=MESH
            ).start()
            return carry

        lax.fori_loop(1, N_DP, body, 0)
        pltpu.make_async_copy(src, dst, sems.at[1]).wait()

    def spread_done(src, dst, sems):
        pltpu.make_async_copy(src.at[pl.ds(0, N_DP - 1)], dst.at[pl.ds(0, N_DP - 1)], sems.at[0]).wait()

    spread(tok_ref, mail, mail_sem)
    m = lax.broadcasted_iota(jnp.int32, (CHUNK, N_DP * 8), 0)
    n = lax.broadcasted_iota(jnp.int32, (CHUNK, N_DP * 8), 1)
    row = m & (ROWS - 1)
    pick = ((row >> 1) * 8 + (row & 1) * 2 + (m >> 6) == n).astype(BF16)
    halves = jnp.dot(pick, mail[...].reshape(N_DP * 8, 128).astype(BF16), preferred_element_type=F32)
    xall[e] = jnp.concatenate([halves[:ROWS], halves[ROWS:]], axis=1).astype(BF16)

    x_copies = {}
    for k, off in enumerate(OFFSETS):
        for c in range(2):
            if k == 0 and c == 0:
                continue
            target = ((Z + off) % NZ) * 2 + (C + c) % 2
            x_copies[BACK[k], c] = send(
                xall.at[e], xall.at[e], x_send.at[k, c], x_recv.at[BACK[k], c], (dp, target)
            )

    for load in loads:
        load.wait()

    def add(ref, value):
        ref[...] = (ref[...].astype(F32) + value.astype(F32)).astype(BF16)

    def x_stage(k, s, piece, buf, base):
        c1 = send(piece(X + 2), buf.at[0], rs_send.at[k, base], rs_recv.at[k, base], at(X + s + NX, Y))
        c2 = send(
            piece(X - s + NX), buf.at[1], rs_send.at[k, base + 1], rs_recv.at[k, base + 1], at(X - s + NX, Y)
        )
        yield
        c1.wait_recv()
        add(buf.at[0], piece(X + s + NX)[...])
        c3 = send(buf.at[0], buf.at[2], rs_send.at[k, base + 2], rs_recv.at[k, base + 2], at(X + s + NX, Y))
        yield
        c2.wait_recv()
        c3.wait_recv()
        return piece(X)[...].astype(F32) + buf[1].astype(F32) + buf[2].astype(F32)

    def y_stage(k, s, piece, buf, base):
        up, down = at(X, Y + s + NY), at(X, Y - s + NY)
        a = b = None
        for step in range(4):
            src = piece(Y + 4) if step == 0 else buf.at[step - 1]
            if step > 0:
                a.wait_recv()
                add(src, piece(Y + (4 - step) * s + NY)[...])
            a = send(src, buf.at[step], rs_send.at[k, base + step], rs_recv.at[k, base + step], up)
            if step < 3:
                src = piece(Y - 3 * s + NY) if step == 0 else buf.at[3 + step]
                if step > 0:
                    b.wait_recv()
                    add(src, piece(Y - (3 - step) * s + NY)[...])
                b = send(
                    src, buf.at[4 + step], rs_send.at[k, base + 4 + step], rs_recv.at[k, base + 4 + step], down
                )
            yield
        a.wait_recv()
        b.wait_recv()
        return piece(Y)[...].astype(F32) + buf[3].astype(F32) + buf[6].astype(F32)

    def strip_at(y):
        return pl.ds(pl.multiple_of(lax.rem(y, NY) * STRIP, STRIP), STRIP)

    def ag_y(k, s, strip, base):
        up, down = at(X, Y + s + NY), at(X, Y - s + NY)
        a = b = None
        for step in range(4):
            if step > 0:
                a.wait_recv()
            ref = strip(Y - step * s + NY)
            a = send(ref, ref, ag_send.at[k, base + step], ag_recv.at[k, base + step], up)
            if step < 3:
                if step > 0:
                    b.wait_recv()
                ref = strip(Y + step * s + NY)
                b = send(ref, ref, ag_send.at[k, base + 4 + step], ag_recv.at[k, base + 4 + step], down)
            yield
        a.wait_recv()
        b.wait_recv()

    def ag_x(k, block, half, base):
        a = send(block(X), block(X), ag_send.at[k, base], ag_recv.at[k, base], at(X + 1, Y))
        b = send(block(X), block(X), ag_send.at[k, base + 1], ag_recv.at[k, base + 1], at(X + NX - 1, Y))
        yield
        a.wait_recv()
        ref = half(X + NX - 1, 0)
        c = send(ref, ref, ag_send.at[k, base + 2], ag_recv.at[k, base + 2], at(X + 1, Y))
        b.wait_recv()
        ref = half(X + 1, 1)
        d = send(ref, ref, ag_send.at[k, base + 3], ag_recv.at[k, base + 3], at(X + NX - 1, Y))
        yield
        c.wait_recv()
        d.wait_recv()

    lane = lax.broadcasted_iota(jnp.int32, (CHUNK, PAD), 1)
    mine = (lane == WIDTH + e) | (lane == WIDTH + N_EXPERT + e)

    def chunk(k):
        off = OFFSETS[k]
        s = 1 if (k // 2) % 2 == 0 else -1
        zc = (Z + off) % NZ
        for c in range(2):
            if (k, c) in x_copies:
                x_copies[k, c].wait_recv()
        x = xall[pl.ds(2 * zc, 2)].reshape(CHUNK, PAD)
        for q in range(NX):
            cols = pl.ds(q * QUARTER, QUARTER)
            part[k, q, :, 0:QUARTER] = jnp.dot(x, wg[:, cols], preferred_element_type=F32).astype(BF16)
            part[k, q, :, QUARTER:] = jnp.dot(x, wu[:, cols], preferred_element_type=F32).astype(BF16)
        i = k // 2
        if k % 2 == 0:
            total = yield from x_stage(k, s, lambda q: part.at[k, lax.rem(q, NX)], xa.at[i], 0)
            xs[i] = total.astype(BF16)
            total = yield from y_stage(k, s, lambda y: xs.at[i, strip_at(y)], xy.at[i], 3)
        else:
            total = yield from y_stage(k, s, lambda y: part.at[k, :, strip_at(y)], ya.at[i], 3)
            yt[i] = total.astype(BF16)
            total = yield from x_stage(k, s, lambda q: yt.at[i, lax.rem(q, NX)], yx.at[i], 0)
        gate, up = total[:, :QUARTER], total[:, QUARTER:]
        hid[k, X, strip_at(Y)] = (gate / (1.0 + jnp.exp(-gate)) * up).astype(BF16)
        if k % 2 == 0:
            half = STRIP // 2
            yield from ag_y(k, s, lambda y: hid.at[k, X, strip_at(y)], 0)
            half = CHUNK // 2
            yield from ag_x(
                k, lambda q: hid.at[k, lax.rem(q, NX)],
                lambda q, h: hid.at[k, lax.rem(q, NX), pl.ds(h * half, half)], 7,
            )
        else:
            def third(q, h):
                return hid.at[k, lax.rem(q, NX), strip_at(Y), pl.ds(h * 128, 128)]

            yield from ag_x(k, lambda q: hid.at[k, lax.rem(q, NX), strip_at(Y)], third, 7)
            yield from ag_y(k, s, lambda y: hid.at[k, :, strip_at(y)], 0)
        o = jnp.dot(hid[k, 0], wd[0:QUARTER, :], preferred_element_type=F32)
        for q in range(1, NX):
            o += jnp.dot(hid[k, q], wd[q * QUARTER:(q + 1) * QUARTER, :], preferred_element_type=F32)
        x = xall[pl.ds(2 * zc, 2)].reshape(CHUNK, PAD)
        weight = jnp.sum(jnp.where(mine, x.astype(F32), 0.0), axis=1, keepdims=True)
        outs[k, :, 0:WIDTH] = (o * weight).astype(BF16)
        for c in range(2):
            target = (C + c) % 2
            rows = outs.at[k, pl.ds(pl.multiple_of(target * ROWS, ROWS), ROWS)]
            if k == 0 and c == 0:
                got[0] = rows[...]
                continue
            o_copies[BACK[k], c] = send(
                rows, got.at[2 * BACK[k] + c], o_send.at[k, c], o_recv.at[BACK[k], c], (dp, zc * 2 + target)
            )

    o_copies = {}
    waiting = [chunk(k) for k in range(NZ)]
    live, slot = [], 0
    while waiting or live:
        if waiting and slot % STAGGER == 0:
            live.append(waiting.pop(0))
        still = []
        for g in live:
            try:
                next(g)
                still.append(g)
            except StopIteration:
                pass
        live = still
        slot += 1

    for key in sorted(o_copies):
        o_copies[key].wait_recv()
    total = got[0].astype(F32)
    for t in range(1, 2 * NZ):
        total += got[t].astype(F32)
    total = total.astype(BF16)
    stacked = jnp.concatenate([total[:, :128], total[:, 128:]], axis=0)
    t = lax.broadcasted_iota(jnp.int32, (N_DP * 8, CHUNK), 0)
    n = lax.broadcasted_iota(jnp.int32, (N_DP * 8, CHUNK), 1)
    sub = t & 7
    place = ((sub < 4) & ((sub & 1) * ROWS + (t >> 3) * 2 + (sub >> 1) == n)).astype(BF16)
    back_src[...] = jnp.dot(place, stacked, preferred_element_type=F32).reshape(N_DP, 8, 128)
    spread(back_src, back, b_sem)
    out_ref[...] = back[...]
    spread_done(tok_ref, mail, mail_sem)
    spread_done(back_src, back, b_sem)
    for copy in sends:
        copy.wait_send()


def shards(tokens, w_gate, w_up, w_down, routes, scores):
    rows = tokens.shape[0]
    weights = ROUTE_SCALE * scores / jnp.sum(scores, axis=1, keepdims=True)
    named = routes[:, :, None] == jnp.arange(N_EXPERT, dtype=jnp.int32)
    table = jnp.sum(jnp.where(named, weights[:, :, None], 0.0), axis=1)
    high = lax.reduce_precision(table, 8, 7)
    low = lax.reduce_precision(table - high, 8, 7)
    extra = jnp.broadcast_to(jnp.concatenate([high, low], axis=1)[:, None, :], (rows, N_DP, PAD - WIDTH))
    tok = jnp.concatenate([tokens.astype(F32).reshape(rows, N_DP, WIDTH), extra], axis=2)
    tok = tok.transpose(1, 0, 2).reshape(N_DP, 2 * rows, 128)
    tok = jnp.pad(tok, ((0, 0), (0, 8 - 2 * rows), (0, 0)))
    dma = pltpu.SemaphoreType.DMA
    vmem = pltpu.VMEM
    half = NZ // 2
    out = pl.pallas_call(
        kernel,
        out_shape=jax.ShapeDtypeStruct((N_DP, 8, 128), F32),
        in_specs=[pl.BlockSpec(memory_space=vmem)] + [pl.BlockSpec(memory_space=pl.ANY)] * 3,
        out_specs=pl.BlockSpec(memory_space=vmem),
        scratch_shapes=[
            vmem((PAD, FFW), BF16),
            vmem((PAD, FFW), BF16),
            vmem((FFW, WIDTH), BF16),
            vmem((N_DP, 8, 128), F32),
            vmem((N_EXPERT, ROWS, PAD), BF16),
            vmem((NZ, NX, CHUNK, 2 * QUARTER), BF16),
            vmem((half, 3, CHUNK, 2 * QUARTER), BF16),
            vmem((half, 7, STRIP, 2 * QUARTER), BF16),
            vmem((half, CHUNK, 2 * QUARTER), BF16),
            vmem((half, 7, NX, STRIP, 2 * QUARTER), BF16),
            vmem((half, NX, STRIP, 2 * QUARTER), BF16),
            vmem((half, 3, STRIP, 2 * QUARTER), BF16),
            vmem((NZ, NX, CHUNK, QUARTER), BF16),
            vmem((NZ, CHUNK, PAD), BF16),
            vmem((2 * NZ, ROWS, PAD), BF16),
            vmem((N_DP, 8, 128), F32),
            vmem((N_DP, 8, 128), F32),
            dma((3,)),
            dma((2,)),
            dma((NZ, 2)),
            dma((NZ, 2)),
            dma((NZ, 10)),
            dma((NZ, 10)),
            dma((NZ, 11)),
            dma((NZ, 11)),
            dma((NZ, 2)),
            dma((NZ, 2)),
            dma((2,)),
        ],
        compiler_params=pltpu.CompilerParams(
            collective_id=0, has_side_effects=True, vmem_limit_bytes=48 * 1024 * 1024
        ),
        name="expert_block",
    )(tok, w_gate, w_up, w_down)
    out = out[:, : 2 * rows].reshape(N_DP, rows, PAD)[:, :, :WIDTH]
    return out.transpose(1, 0, 2).reshape(rows, D).astype(BF16)


def solution(mesh):
    placed = (
        P(("dp", "expert"), None),
        P("expert", "dp", None),
        P("expert", "dp", None),
        P("expert", None, "dp"),
        P(("dp", "expert"), None),
        P(("dp", "expert"), None),
    )
    return jax.shard_map(
        shards, mesh=mesh, in_specs=placed, out_specs=P(("dp", "expert"), None), check_vma=False
    )
```

time: 300 us -> 125 us (0.42)
  waiting for transfers between devices: 181 us -> 0 us
  Pallas kernels: 0 us -> 119 us
  blocking collectives: 75.4 us -> 0 us
  between operations: 13.5 us -> 0.1 us
  starting transfers between devices: 12.9 us -> 0 us
  matrix products: 9.15 us -> 0 us
  local copies, waits for them, and re-layouts: 7.16 us -> 2.94 us
    psum x1 -> x0, waiting for transfers between devices: 164 us -> none  [shards(): lax.psum(up_part.astype(jnp.bfloat16), 'dp').astype(jnp.float32)]
    pallas_call x0 -> x1, Pallas kernels: none -> 119 us  [shards(): pl.pallas_call(kernel, out_shape=jax.ShapeDtypeStruct((N_DP, 8, 128), F32...]
    all_to_all x3 -> x0, blocking collectives: 75.4 us -> none  [the longest x1 29.8 us: shards(): lax.all_to_all(lax.all_to_all(outgoing, 'dp', split_axis=2, concat_axis=2...]
    all_to_all x1 -> x0, waiting for transfers between devices: 16.9 us -> none  [shards(): lax.all_to_all(lax.all_to_all(returning, 'dp', split_axis=2, concat_axis=...]
    all_to_all x1 -> x0, starting transfers between devices: 12.9 us -> none  [shards(): lax.all_to_all(lax.all_to_all(returning, 'dp', split_axis=2, concat_axis=...]
    dot_general x5 -> x0, matrix products: 9.15 us -> none  [the longest x1 3.79 us: shards(): jnp.dot(hidden, down_local, preferred_element_type=jnp.float32)]
  transfers between devices with their start and end apart: 2 -> 0, of which waited for: 2 -> 0; matrix products, arithmetic and copies ran while one was open for 0% -> 0% of each run, Pallas kernels for 0% -> 0%
where the time goes in v1:
time: 125 us; the launch traced here: 124 us
  Pallas kernels  119 us (95%)
  local copies, waits for them, and re-layouts  2.94 us (2%)
  other arithmetic  1.9 us (2%)
    pallas_call x1, Pallas kernels, shards(): pl.pallas_call(kernel, out_shape=jax.ShapeDtypeStruct((N_DP, 8, 128), F32...  119 us

profile of v1, /device:TPU:1, one launch (start us, length us, event | category | flops | bytes accessed | tf_op | source)
XLA Modules:
  0.0 124.4 jit_solution(16171034651512902490)
XLA Ops:
  0.0 0.0 copy-start.3
  0.0 0.0 copy-start.2
  0.0 0.9 reduce_sum.18
  0.9 0.0 copy-done.3
  0.9 0.1 multiply_divide_fusion
  0.9 0.8 select_reduce_fusion
  1.7 0.1 pad_maximum_fusion
  1.8 0.8 reshape.24
  2.7 0.1 copy.10
  2.7 0.1 maximum_bitcast_fusion
  2.8 0.1 reshape.21
  2.9 0.0 copy-done.2
  2.9 0.0 copy-start
  2.9 0.0 copy-start.1
  3.0 0.2 copy.11.wd_hbm
  3.2 0.8 copy-done
  4.0 0.1 copy-done.1
  4.1 119.5 %expert_block.1 = f32[32,8,128]{2,1,0:T(8,128)S(1)} custom-call(f32[32,8,128]{2,1,0:T(8,128)S(1)} %pad.4.tok_ref, bf16[1,224,1024]{2,1,0:T(8,128)(2,1)S(1)} %copy-done, bf16[1,224,1024]{2,1,0:T(8,128)(2,1)S(1)} %copy-done.1, bf16[1,1024,224]{2,1,0:T(8,128)(2,1)S(1)} %copy.11.wd_hbm), custom_call_target="tpu_custom_call" | custom-call | tf_op jit(solution)/shard_map/expert_block/pallas_call | solution.py:296
  123.7 0.7 convert_element_type.11
  (7 shorter events, 0.1 us)
Async XLA Ops:
  0.0 0.9 copy-start.3
  0.0 2.9 %copy-start.2 = (bf16[1,1024,224]{1,2,0:T(8,128)(2,1)S(1)}, bf16[1,1024,224]{1,2,0:T(8,128)(2,1)}, u32[]{:S(2)}) copy-start(bf16[1,1024,224]{1,2,0:T(8,128)(2,1)} %param.9) | copy-start | bytes 1376260
  2.9 1.0 copy-start
  2.9 1.1 copy-start.1

commit v2 on v0

v2 whole, which is shorter than its diff:
```python
import jax
import jax.numpy as jnp
from jax import lax
from jax.experimental import pallas as pl
from jax.experimental.pallas import tpu as pltpu
from jax.sharding import PartitionSpec as P

MESH = pl.DeviceIdType.MESH
F32 = jnp.float32
BF16 = jnp.bfloat16

ROUTE_SCALE = 2.5
NX, NY, NZ = 4, 8, 8
N_DP = NX * NY
N_EXPERT = 2 * NZ
D = 7168
WIDTH = D // N_DP
FFW = 1024
PAD = 256
ROWS = 64
CHUNK = 2 * ROWS
UNITS = FFW // NX
STRIP = CHUNK // NY
SHARE = ROWS // NX
OFFSETS = (0, 1, 7, 2, 6, 3, 5, 4)
BACK = tuple(OFFSETS.index((NZ - o) % NZ) for o in OFFSETS)
ARRIVAL = (10.0, 13.6, 13.6, 18.6, 18.6, 23.6, 23.6, 28.6)
STEPS = (1.3, 6.5, 6.0, 6.0)


def kernel(
    tok_ref, wg_hbm, wu_hbm, wd_hbm, out_ref,
    wg, wu, wd, mail, xall, part, rs, hid, outs, xr, so, got, fin_src, fin,
    mail_sem, w_send, w_recv, x_send, x_recv, s_send, s_recv, rs_send, rs_recv, ag_send, ag_recv,
    xr_send, xr_recv, o_send, o_recv, f_send, f_recv,
):
    dp = lax.axis_index("dp")
    e = lax.axis_index("expert")
    X, Y = dp % NX, dp // NX
    Z, C = e // 2, e % 2
    sibling = (dp, Z * 2 + (C + 1) % 2)

    def at(x, y):
        return (lax.rem(y, NY) * NX + lax.rem(x, NX), e)

    barrier = pltpu.get_barrier_semaphore()

    def greet_dp(j, carry):
        pl.semaphore_signal(barrier, inc=1, device_id=((dp + j) % N_DP, e), device_id_type=MESH)
        return carry

    def greet_expert(j, carry):
        pl.semaphore_signal(barrier, inc=1, device_id=(dp, (e + j) % N_EXPERT), device_id_type=MESH)
        return carry

    lax.fori_loop(1, N_DP, greet_dp, 0)
    lax.fori_loop(1, N_EXPERT, greet_expert, 0)

    wg[:, pl.ds(WIDTH, PAD - WIDTH), :] = jnp.zeros((NX, PAD - WIDTH, UNITS), BF16)
    wu[:, pl.ds(WIDTH, PAD - WIDTH), :] = jnp.zeros((NX, PAD - WIDTH, UNITS), BF16)
    outs[...] = jnp.zeros_like(outs)

    pl.semaphore_wait(barrier, N_DP - 1 + N_EXPERT - 1)

    sends = []

    def send(src, dst, send_sem, recv_sem, device):
        copy = pltpu.make_async_remote_copy(src, dst, send_sem, recv_sem, device_id=device, device_id_type=MESH)
        copy.start()
        sends.append(copy)
        return copy

    own_mail = pltpu.make_async_copy(tok_ref.at[Y], mail.at[dp], mail_sem.at[1])
    own_mail.start()

    def post(j, carry):
        d = (dp + j) % N_DP
        pltpu.make_async_remote_copy(
            tok_ref.at[d // NX], mail.at[dp], mail_sem.at[0], mail_sem.at[1],
            device_id=(d, e), device_id_type=MESH,
        ).start()
        return carry

    lax.fori_loop(1, N_DP, post, 0)

    w_copies = []
    for n, (src, dst) in enumerate(((wg_hbm, wg), (wu_hbm, wu), (wd_hbm, wd))):
        for j in (1, 3, 2, 0):
            x = lax.rem(X + j, NX)
            units = pl.ds(pl.multiple_of(x * UNITS, UNITS), UNITS)
            if n < 2:
                a, b = src.at[0, :, units], dst.at[X, pl.ds(0, WIDTH), :]
            else:
                a, b = src.at[0, units, :], dst.at[X]
            if j == 0:
                copy = pltpu.make_async_copy(a, b, w_recv.at[n, 0])
                copy.start()
                w_copies.append((n, copy.wait))
            else:
                copy = send(a, b, w_send.at[n, j], w_recv.at[n, j], at(x, Y))
                w_copies.append((n, copy.wait_recv))

    pltpu.make_async_copy(mail, mail, mail_sem.at[1]).wait()
    size = N_DP * 16
    m = lax.broadcasted_iota(jnp.int32, (size, size), 0)
    n = lax.broadcasted_iota(jnp.int32, (size, size), 1)
    column, turn = (m >> 4) & 3, (m >> 1) & 7
    pick = ((turn * NX + column) * 16 + (m & 1) * 8 + (m >> 6) == n).astype(BF16)
    rows = jnp.dot(pick, mail[...].reshape(size, 128), preferred_element_type=F32).astype(BF16)
    for b in range(NX):
        for h in range(2):
            t = (2 * b + h) * ROWS
            xall[e, b, :, pl.ds(h * 128, 128)] = rows[t:t + ROWS]

    def pass_on(k, block):
        return send(xall.at[block], xall.at[block], s_send.at[k], s_recv.at[k], sibling)

    s_copies, x_copies = {}, {}
    up, down = (dp, (e + 2) % N_EXPERT), (dp, (e + N_EXPERT - 2) % N_EXPERT)

    def forward(k, block, device):
        x_copies[k] = send(xall.at[block], xall.at[block], x_send.at[k], x_recv.at[k], device)

    s_copies[0] = pass_on(0, e)
    forward(OFFSETS.index(1), e, down)
    forward(OFFSETS.index(7), e, up)

    lane = lax.broadcasted_iota(jnp.int32, (CHUNK, PAD), 1)
    mine = (lane == WIDTH + e) | (lane == WIDTH + N_EXPERT + e)
    o_copies = {}

    def ready(n):
        for kind, wait in w_copies:
            if kind == n:
                wait()

    def strip(y):
        return pl.ds(pl.multiple_of(lax.rem(y, NY) * STRIP, STRIP), STRIP)

    def chunk(k):
        off = OFFSETS[k]
        zc = (Z + off) % NZ
        if k > 0:
            block = zc * 2 + C
            x_copies[k].wait_recv()
            if off in (1, 2):
                forward(OFFSETS.index(off + 1), block, down)
            if off in (7, 6, 5):
                forward(OFFSETS.index(off - 1), block, up)
            s_copies[k] = pass_on(k, block)
        yield
        s_copies[k].wait_recv()
        if k == 0:
            ready(0)
            ready(1)

        def block_rows(b):
            return xall[pl.ds(2 * zc, 2), b].reshape(CHUNK, PAD)

        gate = jnp.dot(block_rows(0), wg[0], preferred_element_type=F32)
        up_ = jnp.dot(block_rows(0), wu[0], preferred_element_type=F32)
        for b in range(1, NX):
            gate += jnp.dot(block_rows(b), wg[b], preferred_element_type=F32)
            up_ += jnp.dot(block_rows(b), wu[b], preferred_element_type=F32)
        part[k, :, 0:UNITS] = gate.astype(BF16)
        part[k, :, UNITS:] = up_.astype(BF16)
        copies = []
        for j in (4, 3, 5, 2, 6, 1, 7):
            copies.append(send(
                part.at[k, strip(Y + j)], rs.at[k, j - 1], rs_send.at[k, j - 1], rs_recv.at[k, j - 1], at(X, Y + j)
            ))
        yield
        for copy in copies:
            copy.wait_recv()
        total = part[k, strip(Y)].astype(F32)
        for j in range(NY - 1):
            total += rs[k, j].astype(F32)
        gate, up_ = total[:, :UNITS], total[:, UNITS:]
        hid[k, strip(Y)] = (gate / (1.0 + jnp.exp(-gate)) * up_).astype(BF16)
        piece = hid.at[k, strip(Y)]
        copies = []
        for j in (4, 3, 5, 2, 6, 1, 7):
            copies.append(send(piece, piece, ag_send.at[k, j - 1], ag_recv.at[k, j - 1], at(X, Y + j)))
        yield
        for copy in copies:
            copy.wait_recv()
        if k == 0:
            ready(2)
        weight = jnp.sum(jnp.where(mine, block_rows(0).astype(F32), 0.0), axis=1, keepdims=True)
        for b in range(NX):
            o = jnp.dot(hid[k], wd[b], preferred_element_type=F32) * weight
            o = o.astype(BF16)
            outs[k, 0, b, :, 0:WIDTH] = o[:ROWS]
            outs[k, 1, b, :, 0:WIDTH] = o[ROWS:]

        def share(x):
            return pl.ds(pl.multiple_of(lax.rem(x, NX) * SHARE, SHARE), SHARE)

        copies = []
        for j in (2, 1, 3):
            copies.append(send(
                outs.at[k, :, :, share(X + j)], xr.at[k, j - 1], xr_send.at[k, j - 1], xr_recv.at[k, j - 1],
                at(X + j, Y),
            ))
        yield
        for copy in copies:
            copy.wait_recv()
        total = outs[k, :, :, share(X)].astype(F32)
        for j in range(NX - 1):
            total += xr[k, j].astype(F32)
        so[k] = total.astype(BF16)
        for c in range(2):
            target = (C + c) % 2
            if k == 0 and c == 0:
                got[0] = so[0, C]
                continue
            o_copies[BACK[k], c] = send(
                so.at[k, target], got.at[2 * BACK[k] + c], o_send.at[k, c], o_recv.at[BACK[k], c],
                (dp, zc * 2 + target),
            )

    events = []
    for k in range(NZ):
        when = ARRIVAL[k]
        events.append((when, k))
        for step in STEPS:
            when += step
            events.append((when, k))
    chunks = [chunk(k) for k in range(NZ)]
    for _, k in sorted(events):
        next(chunks[k], None)

    for key in sorted(o_copies):
        o_copies[key].wait_recv()
    total = got[0].astype(F32)
    for t in range(1, 2 * NZ):
        total += got[t].astype(F32)
    total = total.astype(BF16)
    stacked = jnp.concatenate(
        [total[b, :, h * 128:(h + 1) * 128] for b in range(NX) for h in range(2)], axis=0
    )
    m = lax.broadcasted_iota(jnp.int32, (NY * 16, NY * 16), 0)
    n = lax.broadcasted_iota(jnp.int32, (NY * 16, NY * 16), 1)
    place = ((m & 7) * 16 + (m >> 4) * 2 + ((m >> 3) & 1) == n).astype(BF16)
    moved = jnp.dot(place, stacked, preferred_element_type=F32).astype(BF16)
    fin_src[...] = moved.reshape(NY, 16, 128)
    copies = []
    for j in (4, 3, 5, 2, 6, 1, 7):
        y = lax.rem(Y + j, NY)
        copies.append(send(fin_src.at[y], fin.at[Y], f_send.at[j - 1], f_recv.at[j - 1], at(X, y)))
    fin[Y] = fin_src[Y]
    for copy in copies:
        copy.wait_recv()
    out_ref[...] = fin[...]
    pltpu.make_async_copy(mail.at[pl.ds(0, N_DP - 1)], mail.at[pl.ds(0, N_DP - 1)], mail_sem.at[0]).wait()
    for copy in sends:
        copy.wait_send()


def shards(tokens, w_gate, w_up, w_down, routes, scores):
    rows = tokens.shape[0]
    weights = ROUTE_SCALE * scores / jnp.sum(scores, axis=1, keepdims=True)
    named = routes[:, :, None] == jnp.arange(N_EXPERT, dtype=jnp.int32)
    table = jnp.sum(jnp.where(named, weights[:, :, None], 0.0), axis=1)
    high = lax.reduce_precision(table, 8, 7)
    low = lax.reduce_precision(table - high, 8, 7)
    extra = jnp.concatenate([high, low], axis=1).astype(BF16)[:, None, None, :]
    extra = jnp.broadcast_to(extra, (rows, NY, NX, PAD - WIDTH))
    tok = jnp.concatenate([tokens.reshape(rows, NY, NX, WIDTH), extra], axis=3)
    tok = tok.transpose(1, 0, 2, 3).reshape(NY, 16, 128)
    dma = pltpu.SemaphoreType.DMA
    vmem = pltpu.VMEM
    out = pl.pallas_call(
        kernel,
        out_shape=jax.ShapeDtypeStruct((NY, 16, 128), BF16),
        in_specs=[pl.BlockSpec(memory_space=vmem)] + [pl.BlockSpec(memory_space=pl.ANY)] * 3,
        out_specs=pl.BlockSpec(memory_space=vmem),
        scratch_shapes=[
            vmem((NX, PAD, UNITS), BF16),
            vmem((NX, PAD, UNITS), BF16),
            vmem((NX, UNITS, WIDTH), BF16),
            vmem((N_DP, 16, 128), BF16),
            vmem((N_EXPERT, NX, ROWS, PAD), BF16),
            vmem((NZ, CHUNK, 2 * UNITS), BF16),
            vmem((NZ, NY - 1, STRIP, 2 * UNITS), BF16),
            vmem((NZ, CHUNK, UNITS), BF16),
            vmem((NZ, 2, NX, ROWS, PAD), BF16),
            vmem((NZ, NX - 1, 2, NX, SHARE, PAD), BF16),
            vmem((NZ, 2, NX, SHARE, PAD), BF16),
            vmem((2 * NZ, NX, SHARE, PAD), BF16),
            vmem((NY, 16, 128), BF16),
            vmem((NY, 16, 128), BF16),
            dma((2,)),
            dma((3, NX)),
            dma((3, NX)),
            dma((NZ,)),
            dma((NZ,)),
            dma((NZ,)),
            dma((NZ,)),
            dma((NZ, NY - 1)),
            dma((NZ, NY - 1)),
            dma((NZ, NY - 1)),
            dma((NZ, NY - 1)),
            dma((NZ, NX - 1)),
            dma((NZ, NX - 1)),
            dma((NZ, 2)),
            dma((NZ, 2)),
            dma((NY - 1,)),
            dma((NY - 1,)),
        ],
        compiler_params=pltpu.CompilerParams(
            collective_id=0, has_side_effects=True, vmem_limit_bytes=56 * 1024 * 1024
        ),
        name="expert_block",
    )(tok, w_gate, w_up, w_down)
    out = out.reshape(NY, rows, NX, PAD)[:, :, :, :WIDTH]
    return out.transpose(1, 0, 2, 3).reshape(rows, D)


def solution(mesh):
    placed = (
        P(("dp", "expert"), None),
        P("expert", "dp", None),
        P("expert", "dp", None),
        P("expert", None, "dp"),
        P(("dp", "expert"), None),
        P(("dp", "expert"), None),
    )
    return jax.shard_map(
        shards, mesh=mesh, in_specs=placed, out_specs=P(("dp", "expert"), None), check_vma=False
    )
```

time: 300 us -> 95.9 us (0.32)
  waiting for transfers between devices: 181 us -> 0 us
  Pallas kernels: 0 us -> 89.4 us
  blocking collectives: 75.4 us -> 0 us
  between operations: 13.5 us -> 0.04 us
  starting transfers between devices: 12.9 us -> 0 us
  matrix products: 9.15 us -> 0 us
    psum x1 -> x0, waiting for transfers between devices: 164 us -> none  [shards(): lax.psum(up_part.astype(jnp.bfloat16), 'dp').astype(jnp.float32)]
    pallas_call x0 -> x1, Pallas kernels: none -> 89.4 us  [shards(): pl.pallas_call(kernel, out_shape=jax.ShapeDtypeStruct((NY, 16, 128), BF16...]
    all_to_all x3 -> x0, blocking collectives: 75.4 us -> none  [the longest x1 29.8 us: shards(): lax.all_to_all(lax.all_to_all(outgoing, 'dp', split_axis=2, concat_axis=2...]
    all_to_all x1 -> x0, waiting for transfers between devices: 16.9 us -> none  [shards(): lax.all_to_all(lax.all_to_all(returning, 'dp', split_axis=2, concat_axis=...]
    all_to_all x1 -> x0, starting transfers between devices: 12.9 us -> none  [shards(): lax.all_to_all(lax.all_to_all(returning, 'dp', split_axis=2, concat_axis=...]
    dot_general x5 -> x0, matrix products: 9.15 us -> none  [the longest x1 3.79 us: shards(): jnp.dot(hidden, down_local, preferred_element_type=jnp.float32)]
  transfers between devices with their start and end apart: 2 -> 0, of which waited for: 2 -> 0; matrix products, arithmetic and copies ran while one was open for 0% -> 0% of each run, Pallas kernels for 0% -> 0%
where the time goes in v2:
time: 95.9 us; the launch traced here: 95.6 us
  Pallas kernels  89.4 us (93%)
  local copies, waits for them, and re-layouts  4.29 us (4%)
  other arithmetic  1.88 us (2%)
    pallas_call x1, Pallas kernels, shards(): pl.pallas_call(kernel, out_shape=jax.ShapeDtypeStruct((NY, 16, 128), BF16...  89.4 us
    unnamed x5, local copies, waits for them, and re-layouts  2.02 us

profile of v2, /device:TPU:1, one launch (start us, length us, event | category | flops | bytes accessed | tf_op | source)
XLA Modules:
  0.0 95.6 jit_solution(17792366389054475842)
XLA Ops:
  0.0 0.0 copy-start.1
  0.0 0.0 copy-start
  0.0 0.9 reduce_sum.18
  0.9 0.0 copy-done.1
  0.9 0.1 multiply_divide_fusion
  0.9 0.8 select_reduce_fusion
  1.7 0.1 pad_maximum_fusion
  1.8 0.0 copy-done
  1.8 0.1 reshape.28
  1.9 0.1 maximum_bitcast_fusion
  2.0 0.6 reshape.29.tok_ref
  2.6 2.0 %copy.11.wd_hbm = bf16[1,1024,224]{2,1,0:T(8,128)(2,1)} copy(bf16[1,1024,224]{1,2,0:T(8,128)(2,1)} %param.9) | data formatting | bytes 917504 | tf_op args[3]
  4.6 89.4 %expert_block.1 = bf16[8,16,128]{2,1,0:T(8,128)(2,1)} custom-call(bf16[8,16,128]{2,1,0:T(8,128)(2,1)} %reshape.29.tok_ref, bf16[1,224,1024]{2,1,0:T(8,128)(2,1)} %wg_hbm.1, bf16[1,224,1024]{2,1,0:T(8,128)(2,1)} %wu_hbm.1, bf16[1,1024,224]{2,1,0:T(8,128)(2,1)} %copy.11.wd_hbm), custom_call_target="tpu_custom_call" | custom-call | tf_op jit(solution)/shard_map/expert_block/pallas_call | solution.py:273
  94.0 0.8 reshape.30
  94.8 0.7 reshape.31
  (4 shorter events, 0.0 us)
Async XLA Ops:
  0.0 0.9 copy-start.1
  0.0 1.8 %copy-start = (bf16[2,7168]{1,0:T(2,128)(2,1)S(1)}, bf16[2,7168]{1,0:T(2,128)(2,1)}, u32[]{:S(2)}) copy-start(bf16[2,7168]{1,0:T(2,128)(2,1)} %param.6) | copy-start | bytes 86020

commit v3 on v2

--- a/solution.py
+++ b/solution.py
@@ -16,7 +16,9 @@
 D = 7168
 WIDTH = D // N_DP
 FFW = 1024
-PAD = 256
+SPAN = NX * WIDTH
+GROUPS = SPAN // 128
+PAD = SPAN + 128
 ROWS = 64
 CHUNK = 2 * ROWS
 UNITS = FFW // NX
@@ -29,8 +31,8 @@
 
 
 def kernel(
-    tok_ref, wg_hbm, wu_hbm, wd_hbm, out_ref,
-    wg, wu, wd, mail, xall, part, rs, hid, outs, xr, so, got, fin_src, fin,
+    tok_ref, routes_ref, scores_ref, wg_hbm, wu_hbm, wd_hbm, out_ref,
+    w_in, w_out, tok_src, mail, xall, part, rs, hid, outs, xr, so, got, fin_src, fin,
     mail_sem, w_send, w_recv, x_send, x_recv, s_send, s_recv, rs_send, rs_recv, ag_send, ag_recv,
     xr_send, xr_recv, o_send, o_recv, f_send, f_recv,
 ):
@@ -56,9 +58,19 @@
     lax.fori_loop(1, N_DP, greet_dp, 0)
     lax.fori_loop(1, N_EXPERT, greet_expert, 0)
 
-    wg[:, pl.ds(WIDTH, PAD - WIDTH), :] = jnp.zeros((NX, PAD - WIDTH, UNITS), BF16)
-    wu[:, pl.ds(WIDTH, PAD - WIDTH), :] = jnp.zeros((NX, PAD - WIDTH, UNITS), BF16)
-    outs[...] = jnp.zeros_like(outs)
+    scores = scores_ref[...]
+    weights = ROUTE_SCALE * scores / jnp.sum(scores, axis=1, keepdims=True)
+    routes = routes_ref[...]
+    lanes = lax.broadcasted_iota(jnp.int32, (2, 128), 1)
+    table = jnp.zeros((2, 128), F32)
+    for k in range(routes.shape[1]):
+        table += jnp.where(routes[:, k:k + 1] == (lanes & (N_EXPERT - 1)), weights[:, k:k + 1], 0.0)
+    high = table.astype(BF16).astype(F32)
+    extra = jnp.where(lanes < N_EXPERT, high, jnp.where(lanes < 2 * N_EXPERT, table - high, 0.0))
+    tokens = tok_ref[...].astype(F32)
+    for y in range(NY):
+        pieces = [tokens[:, y * SPAN + g * 128:y * SPAN + (g + 1) * 128] for g in range(GROUPS)]
+        tok_src[y] = jnp.concatenate(pieces + [extra], axis=0).astype(BF16)
 
     pl.semaphore_wait(barrier, N_DP - 1 + N_EXPERT - 1)
 
@@ -70,13 +82,13 @@
         sends.append(copy)
         return copy
 
-    own_mail = pltpu.make_async_copy(tok_ref.at[Y], mail.at[dp], mail_sem.at[1])
+    own_mail = pltpu.make_async_copy(tok_src.at[Y], mail.at[dp], mail_sem.at[1])
     own_mail.start()
 
     def post(j, carry):
         d = (dp + j) % N_DP
         pltpu.make_async_remote_copy(
-            tok_ref.at[d // NX], mail.at[dp], mail_sem.at[0], mail_sem.at[1],
+            tok_src.at[d // NX], mail.at[dp], mail_sem.at[0], mail_sem.at[1],
             device_id=(d, e), device_id_type=MESH,
         ).start()
         return carry
@@ -84,14 +96,12 @@
     lax.fori_loop(1, N_DP, post, 0)
 
     w_copies = []
-    for n, (src, dst) in enumerate(((wg_hbm, wg), (wu_hbm, wu), (wd_hbm, wd))):
+    block = pl.ds(pl.multiple_of(X * WIDTH, 16), WIDTH)
+    homes = (w_in.at[block, pl.ds(0, UNITS)], w_in.at[block, pl.ds(UNITS, UNITS)], w_out.at[block])
+    for n, (src, b) in enumerate(zip((wg_hbm, wu_hbm, wd_hbm), homes)):
         for j in (1, 3, 2, 0):
             x = lax.rem(X + j, NX)
-            units = pl.ds(pl.multiple_of(x * UNITS, UNITS), UNITS)
-            if n < 2:
-                a, b = src.at[0, :, units], dst.at[X, pl.ds(0, WIDTH), :]
-            else:
-                a, b = src.at[0, units, :], dst.at[X]
+            a = src.at[0, :, pl.ds(pl.multiple_of(x * UNITS, UNITS), UNITS)]
             if j == 0:
                 copy = pltpu.make_async_copy(a, b, w_recv.at[n, 0])
                 copy.start()
@@ -105,12 +115,10 @@
     m = lax.broadcasted_iota(jnp.int32, (size, size), 0)
     n = lax.broadcasted_iota(jnp.int32, (size, size), 1)
     column, turn = (m >> 4) & 3, (m >> 1) & 7
-    pick = ((turn * NX + column) * 16 + (m & 1) * 8 + (m >> 6) == n).astype(BF16)
+    pick = ((turn * NX + column) * 16 + (m >> 6) * 2 + (m & 1) == n).astype(BF16)
     rows = jnp.dot(pick, mail[...].reshape(size, 128), preferred_element_type=F32).astype(BF16)
-    for b in range(NX):
-        for h in range(2):
-            t = (2 * b + h) * ROWS
-            xall[e, b, :, pl.ds(h * 128, 128)] = rows[t:t + ROWS]
+    for g in range(GROUPS + 1):
+        xall[e, :, pl.ds(g * 128, 128)] = rows[g * ROWS:(g + 1) * ROWS]
 
     def pass_on(k, block):
         return send(xall.at[block], xall.at[block], s_send.at[k], s_recv.at[k], sibling)
@@ -125,8 +133,8 @@
     forward(OFFSETS.index(1), e, down)
     forward(OFFSETS.index(7), e, up)
 
-    lane = lax.broadcasted_iota(jnp.int32, (CHUNK, PAD), 1)
-    mine = (lane == WIDTH + e) | (lane == WIDTH + N_EXPERT + e)
+    lane = lax.broadcasted_iota(jnp.int32, (CHUNK, 128), 1)
+    mine = (lane == e) | (lane == N_EXPERT + e)
     o_copies = {}
 
     def ready(n):
@@ -154,16 +162,8 @@
             ready(0)
             ready(1)
 
-        def block_rows(b):
-            return xall[pl.ds(2 * zc, 2), b].reshape(CHUNK, PAD)
-
-        gate = jnp.dot(block_rows(0), wg[0], preferred_element_type=F32)
-        up_ = jnp.dot(block_rows(0), wu[0], preferred_element_type=F32)
-        for b in range(1, NX):
-            gate += jnp.dot(block_rows(b), wg[b], preferred_element_type=F32)
-            up_ += jnp.dot(block_rows(b), wu[b], preferred_element_type=F32)
-        part[k, :, 0:UNITS] = gate.astype(BF16)
-        part[k, :, UNITS:] = up_.astype(BF16)
+        x = xall[pl.ds(2 * zc, 2), :, 0:SPAN].reshape(CHUNK, SPAN)
+        part[k] = jnp.dot(x, w_in[...], preferred_element_type=F32).astype(BF16)
         copies = []
         for j in (4, 3, 5, 2, 6, 1, 7):
             copies.append(send(
@@ -186,12 +186,10 @@
             copy.wait_recv()
         if k == 0:
             ready(2)
-        weight = jnp.sum(jnp.where(mine, block_rows(0).astype(F32), 0.0), axis=1, keepdims=True)
-        for b in range(NX):
-            o = jnp.dot(hid[k], wd[b], preferred_element_type=F32) * weight
-            o = o.astype(BF16)
-            outs[k, 0, b, :, 0:WIDTH] = o[:ROWS]
-            outs[k, 1, b, :, 0:WIDTH] = o[ROWS:]
+        extra = xall[pl.ds(2 * zc, 2), :, SPAN:].reshape(CHUNK, 128).astype(F32)
+        weight = jnp.sum(jnp.where(mine, extra, 0.0), axis=1, keepdims=True)
+        o = lax.dot_general(hid[k], w_out[...], (((1,), (1,)), ((), ())), preferred_element_type=F32)
+        outs[k] = (o * weight).astype(BF16).reshape(2, ROWS, SPAN)
 
         def share(x):
             return pl.ds(pl.multiple_of(lax.rem(x, NX) * SHARE, SHARE), SHARE)
@@ -199,13 +197,13 @@
         copies = []
         for j in (2, 1, 3):
             copies.append(send(
-                outs.at[k, :, :, share(X + j)], xr.at[k, j - 1], xr_send.at[k, j - 1], xr_recv.at[k, j - 1],
+                outs.at[k, :, share(X + j)], xr.at[k, j - 1], xr_send.at[k, j - 1], xr_recv.at[k, j - 1],
                 at(X + j, Y),
             ))
         yield
         for copy in copies:
             copy.wait_recv()
-        total = outs[k, :, :, share(X)].astype(F32)
+        total = outs[k, :, share(X)].astype(F32)
         for j in range(NX - 1):
             total += xr[k, j].astype(F32)
         so[k] = total.astype(BF16)
@@ -236,12 +234,10 @@
     for t in range(1, 2 * NZ):
         total += got[t].astype(F32)
     total = total.astype(BF16)
-    stacked = jnp.concatenate(
-        [total[b, :, h * 128:(h + 1) * 128] for b in range(NX) for h in range(2)], axis=0
-    )
-    m = lax.broadcasted_iota(jnp.int32, (NY * 16, NY * 16), 0)
-    n = lax.broadcasted_iota(jnp.int32, (NY * 16, NY * 16), 1)
-    place = ((m & 7) * 16 + (m >> 4) * 2 + ((m >> 3) & 1) == n).astype(BF16)
+    stacked = jnp.concatenate([total[:, g * 128:(g + 1) * 128] for g in range(GROUPS)], axis=0)
+    m = lax.broadcasted_iota(jnp.int32, (NY * 16, GROUPS * 16), 0)
+    n = lax.broadcasted_iota(jnp.int32, (NY * 16, GROUPS * 16), 1)
+    place = (((m >> 1) & 7) * 16 + (m >> 4) * 2 + (m & 1) == n).astype(BF16)
     moved = jnp.dot(place, stacked, preferred_element_type=F32).astype(BF16)
     fin_src[...] = moved.reshape(NY, 16, 128)
     copies = []
@@ -251,43 +247,37 @@
     fin[Y] = fin_src[Y]
     for copy in copies:
         copy.wait_recv()
-    out_ref[...] = fin[...]
+    pieces = []
+    for y in range(NY):
+        tile = fin[y].astype(F32)
+        pieces += [tile[2 * g:2 * g + 2] for g in range(GROUPS)]
+    out_ref[...] = jnp.concatenate(pieces, axis=1).astype(BF16)
     pltpu.make_async_copy(mail.at[pl.ds(0, N_DP - 1)], mail.at[pl.ds(0, N_DP - 1)], mail_sem.at[0]).wait()
     for copy in sends:
         copy.wait_send()
 
 
 def shards(tokens, w_gate, w_up, w_down, routes, scores):
-    rows = tokens.shape[0]
-    weights = ROUTE_SCALE * scores / jnp.sum(scores, axis=1, keepdims=True)
-    named = routes[:, :, None] == jnp.arange(N_EXPERT, dtype=jnp.int32)
-    table = jnp.sum(jnp.where(named, weights[:, :, None], 0.0), axis=1)
-    high = lax.reduce_precision(table, 8, 7)
-    low = lax.reduce_precision(table - high, 8, 7)
-    extra = jnp.concatenate([high, low], axis=1).astype(BF16)[:, None, None, :]
-    extra = jnp.broadcast_to(extra, (rows, NY, NX, PAD - WIDTH))
-    tok = jnp.concatenate([tokens.reshape(rows, NY, NX, WIDTH), extra], axis=3)
-    tok = tok.transpose(1, 0, 2, 3).reshape(NY, 16, 128)
     dma = pltpu.SemaphoreType.DMA
     vmem = pltpu.VMEM
-    out = pl.pallas_call(
+    return pl.pallas_call(
         kernel,
-        out_shape=jax.ShapeDtypeStruct((NY, 16, 128), BF16),
-        in_specs=[pl.BlockSpec(memory_space=vmem)] + [pl.BlockSpec(memory_space=pl.ANY)] * 3,
+        out_shape=jax.ShapeDtypeStruct(tokens.shape, BF16),
+        in_specs=[pl.BlockSpec(memory_space=vmem)] * 3 + [pl.BlockSpec(memory_space=pl.ANY)] * 3,
         out_specs=pl.BlockSpec(memory_space=vmem),
         scratch_shapes=[
-            vmem((NX, PAD, UNITS), BF16),
-            vmem((NX, PAD, UNITS), BF16),
-            vmem((NX, UNITS, WIDTH), BF16),
+            vmem((SPAN, 2 * UNITS), BF16),
+            vmem((SPAN, UNITS), BF16),
+            vmem((NY, 16, 128), BF16),
             vmem((N_DP, 16, 128), BF16),
-            vmem((N_EXPERT, NX, ROWS, PAD), BF16),
+            vmem((N_EXPERT, ROWS, PAD), BF16),
             vmem((NZ, CHUNK, 2 * UNITS), BF16),
             vmem((NZ, NY - 1, STRIP, 2 * UNITS), BF16),
             vmem((NZ, CHUNK, UNITS), BF16),
-            vmem((NZ, 2, NX, ROWS, PAD), BF16),
-            vmem((NZ, NX - 1, 2, NX, SHARE, PAD), BF16),
-            vmem((NZ, 2, NX, SHARE, PAD), BF16),
-            vmem((2 * NZ, NX, SHARE, PAD), BF16),
+            vmem((NZ, 2, ROWS, SPAN), BF16),
+            vmem((NZ, NX - 1, 2, SHARE, SPAN), BF16),
+            vmem((NZ, 2, SHARE, SPAN), BF16),
+            vmem((2 * NZ, SHARE, SPAN), BF16),
             vmem((NY, 16, 128), BF16),
             vmem((NY, 16, 128), BF16),
             dma((2,)),
@@ -312,9 +302,7 @@
             collective_id=0, has_side_effects=True, vmem_limit_bytes=56 * 1024 * 1024
         ),
         name="expert_block",
-    )(tok, w_gate, w_up, w_down)
-    out = out.reshape(NY, rows, NX, PAD)[:, :, :, :WIDTH]
-    return out.transpose(1, 0, 2, 3).reshape(rows, D)
+    )(tokens, routes, scores, w_gate, w_up, w_down.swapaxes(1, 2))
 
 
 def solution(mesh):

time: 95.9 us -> 89.5 us (0.933)
  local copies, waits for them, and re-layouts: 4.29 us -> 1.38 us
  other arithmetic: 1.88 us -> 0 us
  Pallas kernels: 89.4 us -> 87.9 us
    reshape x4 -> x0, local copies, waits for them, and re-layouts: 2.23 us -> none  [the longest x1 0.78 us: shards(): out = out.reshape(NY, rows, NX, PAD)[:, :, :, :WIDTH]]
    reduce_sum x2 -> x0, other arithmetic: 1.63 us -> none  [the longest x1 0.87 us: shards(): weights = ROUTE_SCALE * scores / jnp.sum(scores, axis=1, keepdims=True)]
    pallas_call x1, Pallas kernels: 89.4 us -> 87.9 us  [shards(): pl.pallas_call(kernel, out_shape=jax.ShapeDtypeStruct(tokens.shape, BF16)...]
    unnamed x5 -> x1, local copies, waits for them, and re-layouts: 2.02 us -> 1.38 us
where the time goes in v3:
time: 89.5 us; the launch traced here: 89.3 us
  Pallas kernels  87.9 us (98%)
  local copies, waits for them, and re-layouts  1.38 us (2%)
    pallas_call x1, Pallas kernels, shards(): pl.pallas_call(kernel, out_shape=jax.ShapeDtypeStruct(tokens.shape, BF16)...  87.9 us

profile of v3, /device:TPU:1, one launch (start us, length us, event | category | flops | bytes accessed | tf_op | source)
XLA Modules:
  0.0 89.3 jit_solution(16994309054654031736)
XLA Ops:
  0.0 87.9 %expert_block.1 = bf16[2,7168]{1,0:T(2,128)(2,1)} custom-call(bf16[2,7168]{1,0:T(2,128)(2,1)} %tok_ref.1, s32[2,8]{1,0:T(2,128)} %routes_ref.1, f32[2,8]{1,0:T(2,128)} %scores_ref.1, bf16[1,224,1024]{2,1,0:T(8,128)(2,1)} %wg_hbm.1, bf16[1,224,1024]{2,1,0:T(8,128)(2,1)} %wu_hbm.1, bf16[1,224,1024]{2,1,0:T(8,128)(2,1)} %bitcast.1), custom_call_target="tpu_custom_call" | custom-call | tf_op jit(solution)/shard_map/expert_block/pallas_call | solution.py:263
  87.9 1.4 %copy.8 = bf16[2,7168]{1,0:T(2,128)(2,1)} copy(bf16[2,7168]{1,0:T(2,128)(2,1)} %expert_block.1) | data formatting | bytes 57344

commit v4 on v3

v4 whole, which is shorter than its diff:
```python
import jax
import jax.numpy as jnp
from jax import lax
from jax.experimental import pallas as pl
from jax.experimental.pallas import tpu as pltpu
from jax.sharding import PartitionSpec as P

MESH = pl.DeviceIdType.MESH
F32 = jnp.float32
BF16 = jnp.bfloat16

ROUTE_SCALE = 2.5
NX, NY, NZ = 4, 8, 8
N_DP = NX * NY
N_EXPERT = 2 * NZ
D = 7168
WIDTH = D // N_DP
FFW = 1024
SPAN = NX * WIDTH
GROUPS = SPAN // 128
PAD = SPAN + 128
ROWS = 64
CHUNK = 2 * ROWS
UNITS = FFW // NX
STRIP = CHUNK // NY
SHARE = ROWS // NX
OFFSETS = (0, 1, 7, 2, 6, 3, 5, 4)
BACK = tuple(OFFSETS.index((NZ - o) % NZ) for o in OFFSETS)
STRAIGHT = ()
FAR_FIRST = (4, 3, 5, 2, 6, 1, 7)
FROM_Z = (9.3, 13.3, 13.8, 15.3, 15.8, 17.3, 17.8, 18.8)
FROM_X = (15, 17.5, 18.5, 20, 21, 22, 23, 24)
START = (16.6, 18.9, 19.9, 21.4, 22.6, 24.1, 25.6, 27.1)
HOP = 4.5


def plan():
    events = []
    for k in range(NZ):
        times = [FROM_Z[k], FROM_X[k], START[k]]
        waits = (1.5 * HOP, 1.3 * HOP) if k in STRAIGHT else (HOP,) * 4
        for wait in waits + (1.6, HOP):
            times.append(times[-1] + wait)
        events += [(when, k) for when in times]
    return [k for _, k in sorted(events)]


def kernel(
    tok_ref, routes_ref, scores_ref, wg_hbm, wu_hbm, wd_hbm, out_ref,
    w_in, w_out, tok_src, mail, xall, part, rs, hid, outs, core, so, xr, zs, got, fin_src, fin,
    m_send, m_recv, w_send, w_recv, z_send, z_recv, x_send, x_recv, s_send, s_recv, rs_send, rs_recv, ag_send, ag_recv,
    c_send, c_recv, xr_send, xr_recv, o_send, o_recv, f_send, f_recv,
):
    dp = lax.axis_index("dp")
    e = lax.axis_index("expert")
    X, Y = dp % NX, dp // NX
    Z, C = e // 2, e % 2
    sibling = (dp, Z * 2 + (C + 1) % 2)

    def at(x, y):
        return (lax.rem(y, NY) * NX + lax.rem(x, NX), e)

    barrier = pltpu.get_barrier_semaphore()

    peers = [at(X, Y + j) for j in range(1, NY)] + [sibling]
    peers += [at(X + j, Y) for j in range(1, NX)] + [(dp, lax.rem(e + 2 * j, N_EXPERT)) for j in range(1, NZ)]
    for peer in peers:
        pl.semaphore_signal(barrier, inc=1, device_id=peer, device_id_type=MESH)

    pl.semaphore_wait(barrier, len(peers))

    sends = []

    def send(src, dst, send_sem, recv_sem, device):
        copy = pltpu.make_async_remote_copy(src, dst, send_sem, recv_sem, device_id=device, device_id_type=MESH)
        copy.start()
        sends.append(copy)
        return copy

    w_copies = []
    block = pl.ds(pl.multiple_of(X * WIDTH, 16), WIDTH)
    homes = (w_in.at[block, pl.ds(0, UNITS)], w_in.at[block, pl.ds(UNITS, UNITS)], w_out.at[block])

    def give(n, src, b):
        for j in (2, 1, 3, 0):
            x = lax.rem(X + j, NX)
            a = src.at[0, :, pl.ds(pl.multiple_of(x * UNITS, UNITS), UNITS)]
            if j == 0:
                copy = pltpu.make_async_copy(a, b, w_recv.at[n, 0])
                copy.start()
                w_copies.append((n, copy.wait))
            else:
                copy = send(a, b, w_send.at[n, j], w_recv.at[n, j], at(x, Y))
                w_copies.append((n, copy.wait_recv))

    give(0, wg_hbm, homes[0])
    give(1, wu_hbm, homes[1])

    scores = scores_ref[...]
    weights = ROUTE_SCALE * scores / jnp.sum(scores, axis=1, keepdims=True)
    routes = routes_ref[...]
    lanes = lax.broadcasted_iota(jnp.int32, (2, 128), 1)
    table = jnp.zeros((2, 128), F32)
    for k in range(routes.shape[1]):
        table += jnp.where(routes[:, k:k + 1] == (lanes & (N_EXPERT - 1)), weights[:, k:k + 1], 0.0)
    high = table.astype(BF16).astype(F32)
    extra = jnp.where(lanes < N_EXPERT, high, jnp.where(lanes < 2 * N_EXPERT, table - high, 0.0))
    tokens = tok_ref[...].astype(F32)
    for y in range(NY):
        pieces = [tokens[:, y * SPAN + g * 128:y * SPAN + (g + 1) * 128] for g in range(GROUPS)]
        tok_src[y] = jnp.concatenate(pieces + [extra], axis=0).astype(BF16)

    mail_copies = []
    for j in FAR_FIRST:
        y = lax.rem(Y + j, NY)
        mail_copies.append(send(tok_src.at[y], mail.at[Y], m_send.at[j - 1], m_recv.at[j - 1], at(X, y)))
    mail[Y] = tok_src[Y]

    for copy in mail_copies:
        copy.wait_recv()
    size = NY * 16
    m = lax.broadcasted_iota(jnp.int32, (size, size), 0)
    n = lax.broadcasted_iota(jnp.int32, (size, size), 1)
    pick = (((m >> 1) & 7) * 16 + (m >> 4) * 2 + (m & 1) == n).astype(BF16)
    rows = jnp.dot(pick, mail[...].reshape(size, 128), preferred_element_type=F32).astype(BF16)

    def share(x):
        return pl.ds(pl.multiple_of(lax.rem(x, NX) * SHARE, SHARE), SHARE)

    for g in range(GROUPS + 1):
        xall[e, share(X), pl.ds(g * 128, 128)] = rows[g * SHARE:(g + 1) * SHARE]

    own = xall.at[e, share(X)]
    z_copies = {}
    for k in range(1, NZ):
        there = (dp, lax.rem(e + 2 * OFFSETS[k], N_EXPERT))
        z_copies[BACK[k]] = send(own, own, z_send.at[k], z_recv.at[BACK[k]], there)

    lane = lax.broadcasted_iota(jnp.int32, (CHUNK, 128), 1)
    mine = (lane == e) | (lane == N_EXPERT + e)
    o_copies = {}

    def ready(n):
        for kind, wait in w_copies:
            if kind == n:
                wait()

    def strip(y):
        return pl.ds(pl.multiple_of(lax.rem(y, NY) * STRIP, STRIP), STRIP)

    def sum_send(k, n, src, j):
        return send(src, rs.at[k, n], rs_send.at[k, n], rs_recv.at[k, n], at(X, Y + j + NY))

    def sum_straight(k):
        copies = [sum_send(k, j - 1, part.at[k, strip(Y + j)], j) for j in FAR_FIRST]
        yield
        for copy in copies:
            copy.wait_recv()

    def sum_tree(k, t):
        def piece(j):
            return part.at[k, strip(Y + j + NY)]

        a = sum_send(k, 0, piece(4), 2 * t)
        b = sum_send(k, 1, piece(3 * t), t)
        c = sum_send(k, 2, piece(-3 * t), -t)
        last = [sum_send(k, 3, piece(t), t), sum_send(k, 4, piece(-t), -t)]
        yield
        c.wait_recv()
        rs[k, 2] = (rs[k, 2].astype(F32) + piece(-2 * t)[...].astype(F32)).astype(BF16)
        last.append(sum_send(k, 5, rs.at[k, 2], -2 * t))
        a.wait_recv()
        b.wait_recv()
        total = rs[k, 0].astype(F32) + rs[k, 1].astype(F32) + piece(2 * t)[...].astype(F32)
        rs[k, 0] = total.astype(BF16)
        last.append(sum_send(k, 6, rs.at[k, 0], 2 * t))
        yield
        for copy in last:
            copy.wait_recv()

    def gather_send(k, n, source, j):
        ref = hid.at[k, strip(Y + source + NY)]
        return send(ref, ref, ag_send.at[k, n], ag_recv.at[k, n], at(X, Y + j + NY))

    def gather_straight(k):
        copies = [gather_send(k, j - 1, 0, j) for j in FAR_FIRST]
        yield
        for copy in copies:
            copy.wait_recv()

    def gather_tree(k, t):
        a = gather_send(k, 0, 0, 2 * t)
        b = gather_send(k, 1, 0, -2 * t)
        last = [gather_send(k, 2, 0, t), gather_send(k, 3, 0, -t)]
        yield
        a.wait_recv()
        last.append(gather_send(k, 4, -2 * t, 2 * t))
        last.append(gather_send(k, 5, -2 * t, t))
        b.wait_recv()
        last.append(gather_send(k, 6, 2 * t, -t))
        yield
        for copy in last:
            copy.wait_recv()

    def chunk(k):
        off = OFFSETS[k]
        zc = (Z + off) % NZ
        block = zc * 2 + C
        if k > 0:
            z_copies[k].wait_recv()
        rows = xall.at[block, share(X)]
        copies = []
        for j in (2, 1, 3):
            copies.append(send(rows, rows, x_send.at[k, j - 1], x_recv.at[k, j - 1], at(X + j, Y)))
        if k == NZ - 1:
            give(2, wd_hbm, homes[2])
        yield
        for copy in copies:
            copy.wait_recv()
        copy = send(xall.at[block], xall.at[block], s_send.at[k], s_recv.at[k], sibling)
        yield
        copy.wait_recv()
        if k == 0:
            ready(0)
            ready(1)
        x = xall[pl.ds(2 * zc, 2), :, 0:SPAN].reshape(CHUNK, SPAN)
        part[k] = jnp.dot(x, w_in[...], preferred_element_type=F32).astype(BF16)
        turn = 1 if k % 2 == 0 else -1
        if k in STRAIGHT:
            yield from sum_straight(k)
            parts = [rs[k, j] for j in range(NY - 1)]
        else:
            yield from sum_tree(k, turn)
            parts = [rs[k, j] for j in (3, 4, 5, 6)]
        total = part[k, strip(Y)].astype(F32)
        for value in parts:
            total += value.astype(F32)
        gate, up_ = total[:, :UNITS], total[:, UNITS:]
        hid[k, strip(Y)] = (gate / (1.0 + jnp.exp(-gate)) * up_).astype(BF16)
        if k in STRAIGHT:
            yield from gather_straight(k)
        else:
            yield from gather_tree(k, turn)
        if k == 0:
            ready(2)
        extra = xall[pl.ds(2 * zc, 2), :, SPAN:].reshape(CHUNK, 128).astype(F32)
        weight = jnp.sum(jnp.where(mine, extra, 0.0), axis=1, keepdims=True)
        o = lax.dot_general(hid[k], w_out[...], (((1,), (1,)), ((), ())), preferred_element_type=F32)
        outs[k] = (o * weight).astype(BF16).reshape(2, ROWS, SPAN)
        copy = send(outs.at[k, lax.rem(C + 1, 2)], core.at[k], c_send.at[k], c_recv.at[k], sibling)
        yield
        copy.wait_recv()
        so[k] = (outs[k, C].astype(F32) + core[k].astype(F32)).astype(BF16)
        copies = []
        for j in (2, 1, 3):
            copies.append(send(
                so.at[k, share(X + j)], xr.at[k, j - 1], xr_send.at[k, j - 1], xr_recv.at[k, j - 1], at(X + j, Y)
            ))
        yield
        for copy in copies:
            copy.wait_recv()
        total = so[k, share(X)].astype(F32)
        for j in range(NX - 1):
            total += xr[k, j].astype(F32)
        if k == 0:
            got[0] = total.astype(BF16)
            return
        zs[k] = total.astype(BF16)
        o_copies[BACK[k]] = send(
            zs.at[k], got.at[BACK[k]], o_send.at[k], o_recv.at[BACK[k]], (dp, lax.rem(e + 2 * off, N_EXPERT))
        )

    chunks = [chunk(k) for k in range(NZ)]
    for k in plan():
        next(chunks[k], None)

    for key in sorted(o_copies):
        o_copies[key].wait_recv()
    total = jnp.zeros((SHARE, SPAN), F32)
    for k in range(NZ):
        total += got[k].astype(F32)
    total = total.astype(BF16)
    stacked = jnp.concatenate([total[:, g * 128:(g + 1) * 128] for g in range(GROUPS)], axis=0)
    m = lax.broadcasted_iota(jnp.int32, (NY * 16, GROUPS * 16), 0)
    n = lax.broadcasted_iota(jnp.int32, (NY * 16, GROUPS * 16), 1)
    place = (((m >> 1) & 7) * 16 + (m >> 4) * 2 + (m & 1) == n).astype(BF16)
    moved = jnp.dot(place, stacked, preferred_element_type=F32).astype(BF16)
    fin_src[...] = moved.reshape(NY, 16, 128)
    copies = []
    for j in FAR_FIRST:
        y = lax.rem(Y + j, NY)
        copies.append(send(fin_src.at[y], fin.at[Y], f_send.at[j - 1], f_recv.at[j - 1], at(X, y)))
    fin[Y] = fin_src[Y]
    for copy in copies:
        copy.wait_recv()
    pieces = []
    for y in range(NY):
        tile = fin[y].astype(F32)
        pieces += [tile[2 * g:2 * g + 2] for g in range(GROUPS)]
    out_ref[...] = jnp.concatenate(pieces, axis=1).astype(BF16)
    for copy in sends:
        copy.wait_send()


def shards(tokens, w_gate, w_up, w_down, routes, scores):
    dma = pltpu.SemaphoreType.DMA
    vmem = pltpu.VMEM
    return pl.pallas_call(
        kernel,
        out_shape=jax.ShapeDtypeStruct(tokens.shape, BF16),
        in_specs=[pl.BlockSpec(memory_space=vmem)] * 3 + [pl.BlockSpec(memory_space=pl.ANY)] * 3,
        out_specs=pl.BlockSpec(memory_space=vmem),
        scratch_shapes=[
            vmem((SPAN, 2 * UNITS), BF16),
            vmem((SPAN, UNITS), BF16),
            vmem((NY, 16, 128), BF16),
            vmem((NY, 16, 128), BF16),
            vmem((N_EXPERT, ROWS, PAD), BF16),
            vmem((NZ, CHUNK, 2 * UNITS), BF16),
            vmem((NZ, NY - 1, STRIP, 2 * UNITS), BF16),
            vmem((NZ, CHUNK, UNITS), BF16),
            vmem((NZ, 2, ROWS, SPAN), BF16),
            vmem((NZ, ROWS, SPAN), BF16),
            vmem((NZ, ROWS, SPAN), BF16),
            vmem((NZ, NX - 1, SHARE, SPAN), BF16),
            vmem((NZ, SHARE, SPAN), BF16),
            vmem((NZ, SHARE, SPAN), BF16),
            vmem((NY, 16, 128), BF16),
            vmem((NY, 16, 128), BF16),
            dma((NY - 1,)),
            dma((NY - 1,)),
            dma((3, NX)),
            dma((3, NX)),
            dma((NZ,)),
            dma((NZ,)),
            dma((NZ, NX - 1)),
            dma((NZ, NX - 1)),
            dma((NZ,)),
            dma((NZ,)),
            dma((NZ, NY - 1)),
            dma((NZ, NY - 1)),
            dma((NZ, NY - 1)),
            dma((NZ, NY - 1)),
            dma((NZ,)),
            dma((NZ,)),
            dma((NZ, NX - 1)),
            dma((NZ, NX - 1)),
            dma((NZ,)),
            dma((NZ,)),
            dma((NY - 1,)),
            dma((NY - 1,)),
        ],
        compiler_params=pltpu.CompilerParams(
            collective_id=0, has_side_effects=True, vmem_limit_bytes=56 * 1024 * 1024
        ),
        name="expert_block",
    )(tokens, routes, scores, w_gate, w_up, w_down.swapaxes(1, 2))


def solution(mesh):
    placed = (
        P(("dp", "expert"), None),
        P("expert", "dp", None),
        P("expert", "dp", None),
        P("expert", None, "dp"),
        P(("dp", "expert"), None),
        P(("dp", "expert"), None),
    )
    return jax.shard_map(
        shards, mesh=mesh, in_specs=placed, out_specs=P(("dp", "expert"), None), check_vma=False
    )
```

time: 89.5 us -> 82.8 us (0.925)
  Pallas kernels: 87.9 us -> 80.3 us
    pallas_call x1, Pallas kernels: 87.9 us -> 80.3 us  [shards(): pl.pallas_call(kernel, out_shape=jax.ShapeDtypeStruct(tokens.shape, BF16)...]
where the time goes in v4:
time: 82.8 us; the launch traced here: 81.7 us
  Pallas kernels  80.3 us (97%)
  local copies, waits for them, and re-layouts  1.38 us (2%)
    pallas_call x1, Pallas kernels, shards(): pl.pallas_call(kernel, out_shape=jax.ShapeDtypeStruct(tokens.shape, BF16)...  80.3 us

profile of v4, /device:TPU:1, one launch (start us, length us, event | category | flops | bytes accessed | tf_op | source)
XLA Modules:
  0.0 81.7 jit_solution(1027758023933574989)
XLA Ops:
  0.0 80.3 %expert_block.1 = bf16[2,7168]{1,0:T(2,128)(2,1)} custom-call(bf16[2,7168]{1,0:T(2,128)(2,1)} %tok_ref.1, s32[2,8]{1,0:T(2,128)} %routes_ref.1, f32[2,8]{1,0:T(2,128)} %scores_ref.1, bf16[1,224,1024]{2,1,0:T(8,128)(2,1)} %wg_hbm.1, bf16[1,224,1024]{2,1,0:T(8,128)(2,1)} %wu_hbm.1, bf16[1,224,1024]{2,1,0:T(8,128)(2,1)} %bitcast.1), custom_call_target="tpu_custom_call" | custom-call | tf_op jit(solution)/shard_map/expert_block/pallas_call | solution.py:308
  80.3 1.4 %copy.8 = bf16[2,7168]{1,0:T(2,128)(2,1)} copy(bf16[2,7168]{1,0:T(2,128)(2,1)} %expert_block.1) | data formatting | bytes 57344

commit v5 on v4

--- a/solution.py
+++ b/solution.py
@@ -24,14 +24,14 @@
 UNITS = FFW // NX
 STRIP = CHUNK // NY
 SHARE = ROWS // NX
-OFFSETS = (0, 1, 7, 2, 6, 3, 5, 4)
+OFFSETS = (0, 1, 4, 3, 5, 2, 6, 7)
 BACK = tuple(OFFSETS.index((NZ - o) % NZ) for o in OFFSETS)
 STRAIGHT = ()
 FAR_FIRST = (4, 3, 5, 2, 6, 1, 7)
-FROM_Z = (9.3, 13.3, 13.8, 15.3, 15.8, 17.3, 17.8, 18.8)
-FROM_X = (15, 17.5, 18.5, 20, 21, 22, 23, 24)
-START = (16.6, 18.9, 19.9, 21.4, 22.6, 24.1, 25.6, 27.1)
-HOP = 4.5
+FROM_Z = (9.3, 13.3, 15.8, 16.6, 16.9, 17.4, 17.7, 18.0)
+FROM_X = (15, 17.5, 20, 21, 21.8, 22.8, 23.8, 24.8)
+START = (16.6, 18.9, 21.4, 22.4, 23.2, 24.2, 25.6, 27.1)
+HOP = 3.8
 
 
 def plan():
@@ -46,9 +46,9 @@
 
 
 def kernel(
-    tok_ref, routes_ref, scores_ref, wg_hbm, wu_hbm, wd_hbm, out_ref,
-    w_in, w_out, tok_src, mail, xall, part, rs, hid, outs, core, so, xr, zs, got, fin_src, fin,
-    m_send, m_recv, w_send, w_recv, z_send, z_recv, x_send, x_recv, s_send, s_recv, rs_send, rs_recv, ag_send, ag_recv,
+    tok_hbm, routes_hbm, scores_hbm, wg_hbm, wu_hbm, wd_hbm, out_ref,
+    tok_ref, routes_ref, scores_ref, w_in, w_out, tok_src, mail, xall, part, rs, hid, outs, core, so, xr, zs, got, fin_src, fin,
+    in_sem, m_send, m_recv, w_send, w_recv, z_send, z_recv, x_send, x_recv, s_send, s_recv, rs_send, rs_recv, ag_send, ag_recv,
     c_send, c_recv, xr_send, xr_recv, o_send, o_recv, f_send, f_recv,
 ):
     dp = lax.axis_index("dp")
@@ -59,6 +59,13 @@
 
     def at(x, y):
         return (lax.rem(y, NY) * NX + lax.rem(x, NX), e)
+
+    loads = [
+        pltpu.make_async_copy(src, dst, in_sem.at[n])
+        for n, (src, dst) in enumerate(((tok_hbm, tok_ref), (routes_hbm, routes_ref), (scores_hbm, scores_ref)))
+    ]
+    for load in loads:
+        load.start()
 
     barrier = pltpu.get_barrier_semaphore()
 
@@ -96,6 +103,8 @@
     give(0, wg_hbm, homes[0])
     give(1, wu_hbm, homes[1])
 
+    for load in loads:
+        load.wait()
     scores = scores_ref[...]
     weights = ROUTE_SCALE * scores / jnp.sum(scores, axis=1, keepdims=True)
     routes = routes_ref[...]
@@ -308,9 +317,12 @@
     return pl.pallas_call(
         kernel,
         out_shape=jax.ShapeDtypeStruct(tokens.shape, BF16),
-        in_specs=[pl.BlockSpec(memory_space=vmem)] * 3 + [pl.BlockSpec(memory_space=pl.ANY)] * 3,
+        in_specs=[pl.BlockSpec(memory_space=pl.ANY)] * 6,
         out_specs=pl.BlockSpec(memory_space=vmem),
         scratch_shapes=[
+            vmem(tokens.shape, tokens.dtype),
+            vmem(routes.shape, routes.dtype),
+            vmem(scores.shape, scores.dtype),
             vmem((SPAN, 2 * UNITS), BF16),
             vmem((SPAN, UNITS), BF16),
             vmem((NY, 16, 128), BF16),
@@ -327,6 +339,7 @@
             vmem((NZ, SHARE, SPAN), BF16),
             vmem((NY, 16, 128), BF16),
             vmem((NY, 16, 128), BF16),
+            dma((3,)),
             dma((NY - 1,)),
             dma((NY - 1,)),
             dma((3, NX)),

time: 82.8 us -> 79.2 us (0.957)
  Pallas kernels: 80.3 us -> 76.7 us
    pallas_call x1, Pallas kernels: 80.3 us -> 76.7 us  [shards(): pl.pallas_call(kernel, out_shape=jax.ShapeDtypeStruct(tokens.shape, BF16)...]
where the time goes in v5:
time: 79.2 us; the launch traced here: 78.1 us
  Pallas kernels  76.7 us (97%)
  local copies, waits for them, and re-layouts  1.38 us (2%)
    pallas_call x1, Pallas kernels, shards(): pl.pallas_call(kernel, out_shape=jax.ShapeDtypeStruct(tokens.shape, BF16)...  76.7 us

profile of v5, /device:TPU:1, one launch (start us, length us, event | category | flops | bytes accessed | tf_op | source)
XLA Modules:
  0.0 78.1 jit_solution(7456626363606333939)
XLA Ops:
  0.0 76.7 %expert_block.1 = bf16[2,7168]{1,0:T(2,128)(2,1)} custom-call(bf16[2,7168]{1,0:T(2,128)(2,1)} %tok_hbm.1, s32[2,8]{1,0:T(2,128)} %routes_hbm.1, f32[2,8]{1,0:T(2,128)} %scores_hbm.1, bf16[1,224,1024]{2,1,0:T(8,128)(2,1)} %wg_hbm.1, bf16[1,224,1024]{2,1,0:T(8,128)(2,1)} %wu_hbm.1, bf16[1,224,1024]{2,1,0:T(8,128)(2,1)} %bitcast.1), custom_call_target="tpu_custom_call" | custom-call | tf_op jit(solution)/shard_map/expert_block/pallas_call | solution.py:317
  76.7 1.4 %copy.8 = bf16[2,7168]{1,0:T(2,128)(2,1)} copy(bf16[2,7168]{1,0:T(2,128)(2,1)} %expert_block.1) | data formatting | bytes 57344

commit v6 on v5

--- a/solution.py
+++ b/solution.py
@@ -28,6 +28,7 @@
 BACK = tuple(OFFSETS.index((NZ - o) % NZ) for o in OFFSETS)
 STRAIGHT = ()
 FAR_FIRST = (4, 3, 5, 2, 6, 1, 7)
+LATEST = 16
 FROM_Z = (9.3, 13.3, 15.8, 16.6, 16.9, 17.4, 17.7, 18.0)
 FROM_X = (15, 17.5, 20, 21, 21.8, 22.8, 23.8, 24.8)
 START = (16.6, 18.9, 21.4, 22.4, 23.2, 24.2, 25.6, 27.1)
@@ -125,12 +126,12 @@
         mail_copies.append(send(tok_src.at[y], mail.at[Y], m_send.at[j - 1], m_recv.at[j - 1], at(X, y)))
     mail[Y] = tok_src[Y]
 
-    for copy in mail_copies:
-        copy.wait_recv()
     size = NY * 16
     m = lax.broadcasted_iota(jnp.int32, (size, size), 0)
     n = lax.broadcasted_iota(jnp.int32, (size, size), 1)
     pick = (((m >> 1) & 7) * 16 + (m >> 4) * 2 + (m & 1) == n).astype(BF16)
+    for copy in mail_copies:
+        copy.wait_recv()
     rows = jnp.dot(pick, mail[...].reshape(size, 128), preferred_element_type=F32).astype(BF16)
 
     def share(x):
@@ -283,6 +284,12 @@
     for k in plan():
         next(chunks[k], None)
 
+    m = lax.broadcasted_iota(jnp.int32, (NY * 16, GROUPS * 16), 0)
+    n = lax.broadcasted_iota(jnp.int32, (NY * 16, GROUPS * 16), 1)
+    place = (((m >> 1) & 7) * 16 + (m >> 4) * 2 + (m & 1) == n).astype(BF16)
+    settled = len(sends) - LATEST
+    for copy in sends[:settled]:
+        copy.wait_send()
     for key in sorted(o_copies):
         o_copies[key].wait_recv()
     total = jnp.zeros((SHARE, SPAN), F32)
@@ -290,9 +297,6 @@
         total += got[k].astype(F32)
     total = total.astype(BF16)
     stacked = jnp.concatenate([total[:, g * 128:(g + 1) * 128] for g in range(GROUPS)], axis=0)
-    m = lax.broadcasted_iota(jnp.int32, (NY * 16, GROUPS * 16), 0)
-    n = lax.broadcasted_iota(jnp.int32, (NY * 16, GROUPS * 16), 1)
-    place = (((m >> 1) & 7) * 16 + (m >> 4) * 2 + (m & 1) == n).astype(BF16)
     moved = jnp.dot(place, stacked, preferred_element_type=F32).astype(BF16)
     fin_src[...] = moved.reshape(NY, 16, 128)
     copies = []
@@ -300,6 +304,8 @@
         y = lax.rem(Y + j, NY)
         copies.append(send(fin_src.at[y], fin.at[Y], f_send.at[j - 1], f_recv.at[j - 1], at(X, y)))
     fin[Y] = fin_src[Y]
+    for copy in sends[settled:-len(copies)]:
+        copy.wait_send()
     for copy in copies:
         copy.wait_recv()
     pieces = []
@@ -307,7 +313,7 @@
         tile = fin[y].astype(F32)
         pieces += [tile[2 * g:2 * g + 2] for g in range(GROUPS)]
     out_ref[...] = jnp.concatenate(pieces, axis=1).astype(BF16)
-    for copy in sends:
+    for copy in copies:
         copy.wait_send()
 
 

time: 79.2 us -> 78.9 us (level)
  no operation moved by 1% of the time
where the time goes in v6:
time: 78.9 us; the launch traced here: 77.9 us
  Pallas kernels  76.5 us (97%)
  local copies, waits for them, and re-layouts  1.38 us (2%)
    pallas_call x1, Pallas kernels, shards(): pl.pallas_call(kernel, out_shape=jax.ShapeDtypeStruct(tokens.shape, BF16)...  76.5 us

profile of v6, /device:TPU:1, one launch (start us, length us, event | category | flops | bytes accessed | tf_op | source)
XLA Modules:
  0.0 77.9 jit_solution(982503056415635467)
XLA Ops:
  0.0 76.5 %expert_block.1 = bf16[2,7168]{1,0:T(2,128)(2,1)} custom-call(bf16[2,7168]{1,0:T(2,128)(2,1)} %tok_hbm.1, s32[2,8]{1,0:T(2,128)} %routes_hbm.1, f32[2,8]{1,0:T(2,128)} %scores_hbm.1, bf16[1,224,1024]{2,1,0:T(8,128)(2,1)} %wg_hbm.1, bf16[1,224,1024]{2,1,0:T(8,128)(2,1)} %wu_hbm.1, bf16[1,224,1024]{2,1,0:T(8,128)(2,1)} %bitcast.1), custom_call_target="tpu_custom_call" | custom-call | tf_op jit(solution)/shard_map/expert_block/pallas_call | solution.py:323
  76.5 1.4 %copy.8 = bf16[2,7168]{1,0:T(2,128)(2,1)} copy(bf16[2,7168]{1,0:T(2,128)(2,1)} %expert_block.1) | data formatting | bytes 57344

commit v7 on v6

--- a/solution.py
+++ b/solution.py
@@ -70,8 +70,10 @@
 
     barrier = pltpu.get_barrier_semaphore()
 
-    peers = [at(X, Y + j) for j in range(1, NY)] + [sibling]
-    peers += [at(X + j, Y) for j in range(1, NX)] + [(dp, lax.rem(e + 2 * j, N_EXPERT)) for j in range(1, NZ)]
+    peers = []
+    for j in (4, 3, 5, 2, 6, 1, 7):
+        peers += [at(X, Y + j), (dp, lax.rem(e + 2 * j, N_EXPERT))]
+    peers += [at(X + j, Y) for j in (2, 1, 3)] + [sibling]
     for peer in peers:
         pl.semaphore_signal(barrier, inc=1, device_id=peer, device_id_type=MESH)
 

time: 78.9 us -> 79.1 us (level)
  no operation moved by 1% of the time
where the time goes in v7:
time: 79.1 us; the launch traced here: 77.7 us
  Pallas kernels  76.3 us (96%)
  local copies, waits for them, and re-layouts  1.38 us (2%)
    pallas_call x1, Pallas kernels, shards(): pl.pallas_call(kernel, out_shape=jax.ShapeDtypeStruct(tokens.shape, BF16)...  76.3 us

profile of v7, /device:TPU:1, one launch (start us, length us, event | category | flops | bytes accessed | tf_op | source)
XLA Modules:
  0.0 77.7 jit_solution(18309932248746814593)
XLA Ops:
  0.0 76.3 %expert_block.1 = bf16[2,7168]{1,0:T(2,128)(2,1)} custom-call(bf16[2,7168]{1,0:T(2,128)(2,1)} %tok_hbm.1, s32[2,8]{1,0:T(2,128)} %routes_hbm.1, f32[2,8]{1,0:T(2,128)} %scores_hbm.1, bf16[1,224,1024]{2,1,0:T(8,128)(2,1)} %wg_hbm.1, bf16[1,224,1024]{2,1,0:T(8,128)(2,1)} %wu_hbm.1, bf16[1,224,1024]{2,1,0:T(8,128)(2,1)} %bitcast.1), custom_call_target="tpu_custom_call" | custom-call | tf_op jit(solution)/shard_map/expert_block/pallas_call | solution.py:325
  76.3 1.4 %copy.8 = bf16[2,7168]{1,0:T(2,128)(2,1)} copy(bf16[2,7168]{1,0:T(2,128)(2,1)} %expert_block.1) | data formatting | bytes 57344
